TPU v7x, 32 devices: a whole 2x2x4 slice. The times are simulated.
32 devices in a mesh: pp: 2 (over y), fsdp: 16 (over z, x, core).
Axes of the slice: x: 2, y: 2, z: 4, core: 2. Of those that a mesh axis runs over, the one named last changes fastest.
Arguments:
- inputs: bfloat16 [2, 2048, 2048], P(None, 'fsdp'), may hold values from -6 to 6
- cotangent: bfloat16 [2, 2048, 2048], P(None, 'fsdp'), may hold values from -0.125 to 0.125
- gains: bfloat16 [2, 2048], P('pp', 'fsdp'), may hold values from 0.5 to 1.5
- w_qkv: bfloat16 [2, 2048, 1536], P('pp', 'fsdp'), may hold values from -0.125 to 0.125
- w_out: bfloat16 [2, 2048, 1024], P('pp', 'fsdp'), may hold values from -0.5 to 0.5
Outputs:
- section_out: bfloat16 [2, 2, 2048, 2048], P('pp', None, 'fsdp')
- grad_qkv: float32 [2, 2048, 1536], P('pp', 'fsdp')
- grad_out: float32 [2, 2048, 1024], P('pp', 'fsdp')
- grad_gain: float32 [2, 2048], P('pp', 'fsdp')
All inputs are finite; a program needn't handle non-finite values.
Results may differ from a plain program's by a relative error of at most 0.02.
Values may be sent and summed in bfloat16 or wider, within the bound.
A program may use at most 128 MiB of HBM per device.

v0:
```python
import jax
import jax.numpy as jnp
from jax import lax
from jax.sharding import PartitionSpec as P

HEADS = 16
KV_HEADS = 4
HEAD_DIM = 64


def shifted(value, axis, steps):
    count = lax.axis_size(axis)
    leading, last = (max(0, -steps), min(count, count - steps))
    return lax.ppermute(value, axis, [(source, source + steps) for source in range(leading, last)])


def mix(form, left, right):
    return jnp.einsum(form, left, right, preferred_element_type=jnp.float32)


def rope_tables(length):
    positions = jnp.arange(length, dtype=jnp.float32)
    freqs = 500000.0 ** (-jnp.arange(HEAD_DIM // 2, dtype=jnp.float32) * 2.0 / HEAD_DIM)
    angles = positions[:, None] * freqs[None, :]
    cosine = jnp.concatenate([jnp.cos(angles), jnp.cos(angles)], axis=1)
    sine = jnp.concatenate([jnp.sin(angles), jnp.sin(angles)], axis=1)
    return (cosine, sine)


def rotate_half(values):
    first = values[..., : HEAD_DIM // 2]
    second = values[..., HEAD_DIM // 2 :]
    return jnp.concatenate([-second, first], axis=-1)


def apply_rope(values, cosine, sine):
    return values * cosine[:, None, :] + rotate_half(values) * sine[:, None, :]


def undo_rope(grads, cosine, sine):
    return grads * cosine[:, None, :] - rotate_half(grads * sine[:, None, :])


def layer_forward(layer_in, gain, w_qkv, w_out, cosine, sine):
    length = layer_in.shape[0]
    group = HEADS // KV_HEADS
    inner = HEADS * HEAD_DIM
    kv_width = KV_HEADS * HEAD_DIM
    values = layer_in.astype(jnp.float32)
    scale_inv = lax.rsqrt(jnp.mean(values * values, axis=-1, keepdims=True) + 1e-05)
    normed = (values * scale_inv * gain.astype(jnp.float32)).astype(jnp.bfloat16)
    joined = jnp.dot(normed, w_qkv, preferred_element_type=jnp.float32)
    queries = apply_rope(joined[:, :inner].reshape(length, HEADS, HEAD_DIM), cosine, sine).astype(
        jnp.bfloat16
    )
    keys = apply_rope(
        joined[:, inner : inner + kv_width].reshape(length, KV_HEADS, HEAD_DIM), cosine, sine
    ).astype(jnp.bfloat16)
    values_v = (
        joined[:, inner + kv_width :].reshape(length, KV_HEADS, HEAD_DIM).astype(jnp.bfloat16)
    )
    grouped = queries.reshape(length, KV_HEADS, group, HEAD_DIM)
    scores = mix("skgh,tkh->kgst", grouped, keys) * HEAD_DIM ** (-0.5)
    causal = jnp.arange(length)[:, None] >= jnp.arange(length)[None, :]
    weights = jnp.where(causal, jnp.exp(scores), 0.0)
    probs = (weights / jnp.sum(weights, axis=-1, keepdims=True)).astype(jnp.bfloat16)
    context = mix("kgst,tkh->skgh", probs, values_v).reshape(length, inner).astype(jnp.bfloat16)
    mixed = values + mix("sc,dc->sd", context, w_out)
    saved = (values, scale_inv, normed, grouped, keys, values_v, probs, context)
    return (mixed.astype(jnp.bfloat16), saved)


def layer_backward(grad_in, saved, gain, w_qkv, w_out, cosine, sine):
    values, scale_inv, normed, grouped, keys, values_v, probs, context = saved
    length = grad_in.shape[0]
    group = HEADS // KV_HEADS
    inner = HEADS * HEAD_DIM
    kv_width = KV_HEADS * HEAD_DIM
    grad_ctx = jnp.dot(grad_in, w_out, preferred_element_type=jnp.float32).astype(jnp.bfloat16)
    grad_ctx = grad_ctx.reshape(length, KV_HEADS, group, HEAD_DIM)
    grad_probs = mix("skgh,tkh->kgst", grad_ctx, values_v)
    grad_values = mix("kgst,skgh->tkh", probs, grad_ctx)
    probs_wide = probs.astype(jnp.float32)
    grad_scores = probs_wide * (
        grad_probs - jnp.sum(grad_probs * probs_wide, axis=-1, keepdims=True)
    )
    grad_scores = (grad_scores * HEAD_DIM ** (-0.5)).astype(jnp.bfloat16)
    grad_queries = mix("kgst,tkh->skgh", grad_scores, keys).reshape(length, HEADS, HEAD_DIM)
    grad_keys = mix("kgst,skgh->tkh", grad_scores, grouped)
    grad_joined = jnp.concatenate(
        [
            undo_rope(grad_queries, cosine, sine).reshape(length, inner),
            undo_rope(grad_keys, cosine, sine).reshape(length, kv_width),
            grad_values.reshape(length, kv_width),
        ],
        axis=1,
    ).astype(jnp.bfloat16)
    grad_normed = mix("sj,dj->sd", grad_joined, w_qkv)
    scaled = grad_normed * gain.astype(jnp.float32)
    grad_x = scale_inv * scaled - values * scale_inv**3 * jnp.mean(
        scaled * values, axis=-1, keepdims=True
    )
    grad_x = grad_x + grad_in.astype(jnp.float32)
    return (grad_x.astype(jnp.bfloat16), grad_joined)


def on_device(inputs, cotangent, gains, w_qkv, w_out):
    section_count = lax.axis_size("pp")
    section_index = lax.axis_index("pp")
    full_qkv, full_out, full_gain = (
        lax.all_gather(w_qkv[0], "fsdp", axis=0, tiled=True),
        lax.all_gather(w_out[0], "fsdp", axis=0, tiled=True),
        lax.all_gather(gains[0], "fsdp", axis=0, tiled=True),
    )
    micro_count, length, width = inputs.shape
    joined_width = full_qkv.shape[1]
    inner = full_out.shape[1]
    tick_count = micro_count + section_count - 1
    last_section = section_count - 1
    cosine, sine = rope_tables(length)

    def forward_tick(carry, tick):
        received, saved_in, outputs = carry
        slot = tick - section_index
        valid = jnp.logical_and(slot >= 0, slot < micro_count)
        slot_index = jnp.clip(slot, 0, micro_count - 1)
        first_in = lax.dynamic_index_in_dim(inputs, slot_index, 0, keepdims=False)
        layer_in = jnp.where(section_index == 0, first_in, received)

        def forward_run_layer(operands):
            current, kept_in, kept_out = operands
            layer_out = layer_forward(current, full_gain, full_qkv, full_out, cosine, sine)[0]
            kept_in = lax.dynamic_update_index_in_dim(kept_in, current, slot_index, 0)
            kept_out = lax.dynamic_update_index_in_dim(kept_out, layer_out, slot_index, 0)
            return (layer_out, kept_in, kept_out)

        def forward_skip_layer(operands):
            current, kept_in, kept_out = operands
            return (jnp.zeros_like(current), kept_in, kept_out)

        layer_out, saved_in, outputs = lax.cond(
            valid, forward_run_layer, forward_skip_layer, (layer_in, saved_in, outputs)
        )
        received = shifted(layer_out, "pp", 1)
        return ((received, saved_in, outputs), None)

    blank = jnp.zeros((micro_count, length, width), jnp.bfloat16)
    start_carry = (jnp.zeros((length, width), jnp.bfloat16), blank, blank)
    (_, saved_in, outputs), _ = lax.scan(forward_tick, start_carry, jnp.arange(tick_count))
    extra = (
        blank,
        jnp.zeros((micro_count, length, inner), jnp.bfloat16),
        jnp.zeros((micro_count, length, joined_width), jnp.bfloat16),
        blank,
    )

    def backward_tick(carry, tick):
        received, kept = carry
        slot = tick - (last_section - section_index)
        valid = jnp.logical_and(slot >= 0, slot < micro_count)
        slot_index = jnp.clip(slot, 0, micro_count - 1)
        last_in = lax.dynamic_index_in_dim(cotangent, slot_index, 0, keepdims=False)
        grad_in = jnp.where(section_index == last_section, last_in, received)

        def backward_run_layer(operands):
            current, store = operands
            layer_in = lax.dynamic_index_in_dim(saved_in, slot_index, 0, keepdims=False)
            saved = layer_forward(layer_in, full_gain, full_qkv, full_out, cosine, sine)[1]
            grad_x, grad_joined = layer_backward(
                current, saved, full_gain, full_qkv, full_out, cosine, sine
            )
            pieces = (saved[2], saved[7], grad_joined, current)
            store = tuple(
                (
                    lax.dynamic_update_index_in_dim(buffer, piece, slot_index, 0)
                    for buffer, piece in zip(store, pieces)
                )
            )
            return (grad_x, store)

        def backward_skip_layer(operands):
            current, store = operands
            return (jnp.zeros_like(current), store)

        grad_x, kept = lax.cond(valid, backward_run_layer, backward_skip_layer, (grad_in, kept))
        received = shifted(grad_x, "pp", -1)
        return ((received, kept), None)

    (_, extra), _ = lax.scan(
        backward_tick, (jnp.zeros((length, width), jnp.bfloat16), extra), jnp.arange(tick_count)
    )
    normed_all, context_all, joined_all, incoming_all = extra
    summed = lax.psum_scatter(
        jnp.concatenate(
            [
                mix("msd,msj->dj", normed_all, joined_all),
                mix("msd,msc->dc", incoming_all, context_all),
            ],
            axis=1,
        ).astype(jnp.bfloat16),
        "fsdp",
        scatter_dimension=0,
        tiled=True,
    ).astype(jnp.float32)
    grad_qkv = summed[:, :joined_width]
    grad_out = summed[:, joined_width:]
    grad_gain = jnp.sum(grad_qkv * w_qkv[0].astype(jnp.float32), axis=1) / gains[0].astype(
        jnp.float32
    )
    return (outputs[None], grad_qkv[None], grad_out[None], grad_gain[None])


def solution(mesh):
    return jax.shard_map(
        on_device,
        mesh=mesh,
        in_specs=(
            P(None, "fsdp", None),
            P(None, "fsdp", None),
            P("pp", "fsdp"),
            P("pp", "fsdp", None),
            P("pp", "fsdp", None),
        ),
        out_specs=(
            P("pp", None, "fsdp", None),
            P("pp", "fsdp", None),
            P("pp", "fsdp", None),
            P("pp", "fsdp"),
        ),
        check_vma=False,
    )
```

profile of v0, /device:TPU:0, one launch (start us, length us, event | category | flops | bytes accessed | tf_op | source)
XLA Modules:
  0.0 538.7 jit_solution(14193623786719429074)
XLA Ops:
  8.7 23.2 %all-gather = bf16[1,2048]{1,0:T(2,128)(2,1)S(1)} all-gather(bf16[1,128]{1,0:T(2,128)(2,1)} %param.15), channel_id=2, replica_groups=mesh['pp'=2,'fsdp'=16] {'fsdp'}, dimensions={1}, use_global_device_ids=true | all-gather | bytes 4352 | tf_op jit(solution)/shard_map/all_gather | solution.py:113
  32.7 30.8 %all-gather.8.cloned.1.call-done = bf16[1,2048,1024]{2,1,0:T(8,128)(2,1)} async-done(((bf16[1,128,1024]{2,1,0:T(8,128)(2,1)}), bf16[1,2048,1024]{2,1,0:T(8,128)(2,1)}) %all-gather.8.cloned.1.call-update) | async-done | bytes 4194320 | tf_op jit(solution)/shard_map/all_gather | solution.py:112
  63.5 62.7 %all-gather.6.cloned.1.call-done = bf16[1,2048,1536]{2,1,0:T(8,128)(2,1)} async-done(((bf16[1,128,1536]{2,1,0:T(8,128)(2,1)}), bf16[1,2048,1536]{2,1,0:T(8,128)(2,1)}) %all-gather.6.cloned.1.call-update) | async-done | bytes 6291472 | tf_op jit(solution)/shard_map/all_gather | solution.py:111
  127.9 97.6 %while.35 = (s32[]{:T(128)}, bf16[128,2048]{1,0:T(8,128)(2,1)S(1)}, bf16[2,128,2048]{2,1,0:T(8,128)(2,1)S(1)}, bf16[2,128,2048]{2,1,0:T(8,128)(2,1)}, s32[3]{0:T...) while((s32[]{:T(128)}, bf16[128,2048]{1,0:T(8,128)(2,1)S(1)}, ...), condition=%wide.region_5.6_spmd, body=%wide.region_0.5_spmd.sunk | while | flops 1414271232 | bytes 26401168 | solution.py:149
  129.8 16.0 %conditional.4 = (bf16[128,2048]{1,0:T(8,128)(2,1)}, bf16[2,128,2048]{2,1,0:T(8,128)(2,1)S(1)}, bf16[2,128,2048]{2,1,0:T(8,128)(2,1)}) conditional(s32[]{:T(128)} %convert_element_type.295, (bf16[2,128,2048]{2,1,0:T(8,128)(2,1)S(1)}, bf16[2,128,2048]{2,1,0:T(8,128)(2,1)}) %tuple.93, (pred[]{:T(512)}, s32[]{:T(128)}, bf16[2,128,2048]{2,1,0:T(8,128)(2,1)}, ...), branch_computations={%region_1.1_spmd, %region_2.4_spmd} | conditional | flops 1414271232 | bytes 24303672 | solution.py:141
  131.9 3.8 fusion.7
  139.2 1.8 convolution_convert_fusion
  141.1 4.7 bitcast_dynamic-update-slice_fusion
  147.1 12.1 %collective-permute-done = bf16[128,2048]{1,0:T(8,128)(2,1)S(1)} collective-permute-done((bf16[128,2048]{1,0:T(8,128)(2,1)}, bf16[128,2048]{1,0:T(8,128)(2,1)S(1)}, u32[]{:S(2)}, u32[]{:S(2)}) %collective-permute-start) | collective-permute-done | bytes 524320 | tf_op jit(solution)/shard_map/while/body/eval_jaxpr/ppermute | solution.py:14
  161.1 16.0 %conditional.4 = (bf16[128,2048]{1,0:T(8,128)(2,1)}, bf16[2,128,2048]{2,1,0:T(8,128)(2,1)S(1)}, bf16[2,128,2048]{2,1,0:T(8,128)(2,1)}) conditional(s32[]{:T(128)} %convert_element_type.295, (bf16[2,128,2048]{2,1,0:T(8,128)(2,1)S(1)}, bf16[2,128,2048]{2,1,0:T(8,128)(2,1)}) %tuple.93, (pred[]{:T(512)}, s32[]{:T(128)}, bf16[2,128,2048]{2,1,0:T(8,128)(2,1)}, ...), branch_computations={%region_1.1_spmd, %region_2.4_spmd} | conditional | flops 1414271232 | bytes 24303672 | solution.py:141
  163.3 3.8 fusion.7
  169.2 1.3 fusion.3
  170.6 1.8 convolution_convert_fusion
  172.4 4.7 bitcast_dynamic-update-slice_fusion
  177.1 4.3 collective-permute-start
  181.4 11.4 %collective-permute-done = bf16[128,2048]{1,0:T(8,128)(2,1)S(1)} collective-permute-done((bf16[128,2048]{1,0:T(8,128)(2,1)}, bf16[128,2048]{1,0:T(8,128)(2,1)S(1)}, u32[]{:S(2)}, u32[]{:S(2)}) %collective-permute-start) | collective-permute-done | bytes 524320 | tf_op jit(solution)/shard_map/while/body/eval_jaxpr/ppermute | solution.py:14
  195.5 19.4 %collective-permute-start = (bf16[128,2048]{1,0:T(8,128)(2,1)}, bf16[128,2048]{1,0:T(8,128)(2,1)S(1)}, u32[]{:S(2)}, u32[]{:S(2)}) collective-permute-start(bf16[128,2048]{1,0:T(8,128)(2,1)} %get-tuple-element.805), channel_id=1, source_target_pairs={{0,16},{1,17},{2,18},{3,19},{4,20},{5,21},{6,22},{7,23},{8,24},{9,... | collective-permute-start | bytes 1572872 | tf_op jit(solution)/shard_map/while/body/eval_jaxpr/ppermute | solution.py:14
  214.9 10.5 %collective-permute-done = bf16[128,2048]{1,0:T(8,128)(2,1)S(1)} collective-permute-done((bf16[128,2048]{1,0:T(8,128)(2,1)}, bf16[128,2048]{1,0:T(8,128)(2,1)S(1)}, u32[]{:S(2)}, u32[]{:S(2)}) %collective-permute-start) | collective-permute-done | bytes 524320 | tf_op jit(solution)/shard_map/while/body/eval_jaxpr/ppermute | solution.py:14
  230.1 148.4 %while.36 = (s32[]{:T(128)}, bf16[128,2048]{1,0:T(8,128)(2,1)S(1)}, bf16[2,128,2048]{2,1,0:T(8,128)(2,1)}, bf16[2,128,1024]{1,2,0:T(8,128)(2,1)}, bf16[2,128,153...) while((s32[]{:T(128)}, bf16[128,2048]{1,0:T(8,128)(2,1)S(1)}, ...), condition=%wide.region_13.14_spmd, body=%wide.region_6.13_spmd.sunk | while | flops 2399433728 | bytes 56126648 | solution.py:189
  234.3 46.0 %collective-permute-done.1 = bf16[128,2048]{1,0:T(8,128)(2,1)S(1)} collective-permute-done((bf16[128,2048]{1,0:T(8,128)(2,1)}, bf16[128,2048]{1,0:T(8,128)(2,1)S(1)}, u32[]{:S(2)}, u32[]{:S(2)}) %collective-permute-start.1) | collective-permute-done | bytes 524320 | tf_op jit(solution)/shard_map/while/body/eval_jaxpr/ppermute | solution.py:14
  282.3 34.3 %conditional.5 = (bf16[128,2048]{1,0:T(8,128)(2,1)}, bf16[2,128,2048]{2,1,0:T(8,128)(2,1)}, bf16[2,128,1024]{1,2,0:T(8,128)(2,1)}, bf16[2,128,1536]{1,2,0:T(8,128)(2,1)}, bf16[2,128,2048]{2,1,0:T(8,128)(2,1)}) conditional(s32[]{:T(128)} %convert_element_type.296, (bf16[2,128,2048]{2,1,0:T(8,128)(2,1)}, bf16[2,128,1024]{1,2,0:T(8,128)(2,1)}, ...), branch_computations={%region_7.7_spmd, %region_8.12_spmd} | conditional | flops 2399433728 | bytes 54029088 | solution.py:185
  283.2 2.4 bitcast_dynamic-update-slice_fusion.2
  285.6 2.9 convolution_convert_fusion.2
  289.4 3.8 fusion.53
  295.4 1.9 fusion.41
  298.9 2.3 convolution_bitcast_fusion
  301.2 2.2 divide_convert_fusion.1
  303.5 2.3 broadcast_multiply_fusion
  305.8 2.3 fusion.39
  308.4 5.1 fusion.49
  317.9 12.0 %collective-permute-done.1 = bf16[128,2048]{1,0:T(8,128)(2,1)S(1)} collective-permute-done((bf16[128,2048]{1,0:T(8,128)(2,1)}, bf16[128,2048]{1,0:T(8,128)(2,1)S(1)}, u32[]{:S(2)}, u32[]{:S(2)}) %collective-permute-start.1) | collective-permute-done | bytes 524320 | tf_op jit(solution)/shard_map/while/body/eval_jaxpr/ppermute | solution.py:14
  331.9 34.3 %conditional.5 = (bf16[128,2048]{1,0:T(8,128)(2,1)}, bf16[2,128,2048]{2,1,0:T(8,128)(2,1)}, bf16[2,128,1024]{1,2,0:T(8,128)(2,1)}, bf16[2,128,1536]{1,2,0:T(8,128)(2,1)}, bf16[2,128,2048]{2,1,0:T(8,128)(2,1)}) conditional(s32[]{:T(128)} %convert_element_type.296, (bf16[2,128,2048]{2,1,0:T(8,128)(2,1)}, bf16[2,128,1024]{1,2,0:T(8,128)(2,1)}, ...), branch_computations={%region_7.7_spmd, %region_8.12_spmd} | conditional | flops 2399433728 | bytes 54029088 | solution.py:185
  332.8 2.4 bitcast_dynamic-update-slice_fusion.2
  335.2 2.9 convolution_convert_fusion.2
  338.9 3.8 fusion.53
  345.0 1.9 fusion.41
  348.5 2.3 convolution_bitcast_fusion
  350.8 2.2 divide_convert_fusion.1
  353.1 2.3 broadcast_multiply_fusion
  355.4 2.3 fusion.39
  357.9 5.1 fusion.49
  367.5 11.0 %collective-permute-done.1 = bf16[128,2048]{1,0:T(8,128)(2,1)S(1)} collective-permute-done((bf16[128,2048]{1,0:T(8,128)(2,1)}, bf16[128,2048]{1,0:T(8,128)(2,1)S(1)}, u32[]{:S(2)}, u32[]{:S(2)}) %collective-permute-start.1) | collective-permute-done | bytes 524320 | tf_op jit(solution)/shard_map/while/body/eval_jaxpr/ppermute | solution.py:14
  378.5 2.6 bitcast_convert_fusion.1
  381.1 3.3 bitcast_convert_fusion
  384.4 12.6 %pad_maximum_fusion.1 = bf16[2048,2560]{0,1:T(8,128)(2,1)} fusion(bf16[2048,1024]{0,1:T(8,128)(2,1)S(1)} %bitcast_convert_fusion.1, bf16[2048,1536]{0,1:T(8,128)(2,1)S(1)} %bitcast_convert_fusion), kind=kLoop, calls=%fused_computation.127 | loop fusion | flops 20971520 | bytes 20971520 | tf_op jit(solution)/shard_map/concatenate | solution.py:194
  397.0 13.7 %copy.79 = bf16[2048,2560]{1,0:T(8,128)(2,1)} copy(bf16[2048,2560]{0,1:T(8,128)(2,1)} %pad_maximum_fusion.1) | data formatting | bytes 20971520
  411.9 115.8 %reduce-scatter.4.cloned.1.call-done = bf16[128,2560]{1,0:T(8,128)(2,1)} async-done(((bf16[2048,2560]{1,0:T(8,128)(2,1)}), bf16[128,2560]{1,0:T(8,128)(2,1)}) %reduce-scatter.4.cloned.1.call-update) | async-done | bytes 655376
  527.7 1.4 copy.80
  (154 shorter events, 56.5 us)
Async XLA Ops:
  7.2 56.3 %all-gather.8.cloned.1.call-start = ((), (), s32[]{:S(2)}) async-start(), calls=%async_computation.2 | async-start | bytes 4456448 | tf_op jit(solution)/shard_map/all_gather | solution.py:112
  7.9 118.2 %all-gather.6.cloned.1.call-start = ((), (), s32[]{:S(2)}) async-start(), calls=%async_computation.1 | async-start | bytes 6684672 | tf_op jit(solution)/shard_map/all_gather | solution.py:111
  8.6 519.0 %reduce-scatter.4.cloned.1.call-start = ((), (), s32[]{:S(2)}) async-start(), calls=%async_computation.3 | async-start | bytes 11141120
  145.8 13.5 %collective-permute-start = (bf16[128,2048]{1,0:T(8,128)(2,1)}, bf16[128,2048]{1,0:T(8,128)(2,1)S(1)}, u32[]{:S(2)}, u32[]{:S(2)}) collective-permute-start(bf16[128,2048]{1,0:T(8,128)(2,1)} %get-tuple-element.805), channel_id=1, source_target_pairs={{0,16},{1,17},{2,18},{3,19},{4,20},{5,21},{6,22},{7,23},{8,24},{9,... | collective-permute-start | bytes 1572872 | tf_op jit(solution)/shard_map/while/body/eval_jaxpr/ppermute | solution.py:14
  177.1 15.7 %collective-permute-start = (bf16[128,2048]{1,0:T(8,128)(2,1)}, bf16[128,2048]{1,0:T(8,128)(2,1)S(1)}, u32[]{:S(2)}, u32[]{:S(2)}) collective-permute-start(bf16[128,2048]{1,0:T(8,128)(2,1)} %get-tuple-element.805), channel_id=1, source_target_pairs={{0,16},{1,17},{2,18},{3,19},{4,20},{5,21},{6,22},{7,23},{8,24},{9,... | collective-permute-start | bytes 1572872 | tf_op jit(solution)/shard_map/while/body/eval_jaxpr/ppermute | solution.py:14
  195.5 29.9 %collective-permute-start = (bf16[128,2048]{1,0:T(8,128)(2,1)}, bf16[128,2048]{1,0:T(8,128)(2,1)S(1)}, u32[]{:S(2)}, u32[]{:S(2)}) collective-permute-start(bf16[128,2048]{1,0:T(8,128)(2,1)} %get-tuple-element.805), channel_id=1, source_target_pairs={{0,16},{1,17},{2,18},{3,19},{4,20},{5,21},{6,22},{7,23},{8,24},{9,... | collective-permute-start | bytes 1572872 | tf_op jit(solution)/shard_map/while/body/eval_jaxpr/ppermute | solution.py:14
  233.0 47.3 %collective-permute-start.1 = (bf16[128,2048]{1,0:T(8,128)(2,1)}, bf16[128,2048]{1,0:T(8,128)(2,1)S(1)}, u32[]{:S(2)}, u32[]{:S(2)}) collective-permute-start(bf16[128,2048]{1,0:T(8,128)(2,1)} %get-tuple-element.824), channel_id=1, source_target_pairs={{16,0},{17,1},{18,2},{19,3},{20,4},{21,5},{22,6},{23,7},{24,8},{25... | collective-permute-start | bytes 1572872 | tf_op jit(solution)/shard_map/while/body/eval_jaxpr/ppermute | solution.py:14
  293.4 10.1 %copy-start.3 = (bf16[128,4,64,1]{0,2,3,1:T(8,128)(2,1)}, bf16[128,4,64,1]{0,2,3,1:T(8,128)(2,1)S(1)}, u32[]{:S(2)}) copy-start(bf16[128,4,64,1]{0,2,3,1:T(8,128)(2,1)S(1)} %fusion.73) | copy-start | bytes 196612 | tf_op jit(solution)/shard_map/while/body/eval_jaxpr/cond
  293.8 0.7 copy-start
  294.4 0.6 copy-start.6
  297.9 5.6 %copy-start.1 = (bf16[128,4,4,64]{0,3,2,1:T(8,128)(2,1)S(1)}, bf16[128,4,4,64]{0,3,2,1:T(8,128)(2,1)}, u32[]{:S(2)}) copy-start(bf16[128,4,4,64]{0,3,2,1:T(8,128)(2,1)} %copy-done) | copy-start | bytes 786436 | tf_op jit(solution)/shard_map/while/body/eval_jaxpr/cond
  298.9 6.9 %copy-start.4 = (bf16[128,256]{0,1:T(8,128)(2,1)}, bf16[128,256]{0,1:T(8,128)(2,1)S(1)}, u32[]{:S(2)}) copy-start(bf16[128,256]{0,1:T(8,128)(2,1)S(1)} %copy.59) | copy-start | bytes 196612 | tf_op jit(solution)/shard_map/while/body/eval_jaxpr/cond
  308.4 6.4 %copy-start.5 = (bf16[128,256]{0,1:T(8,128)(2,1)S(1)}, bf16[128,256]{0,1:T(8,128)(2,1)}, u32[]{:S(2)}) copy-start(bf16[128,256]{0,1:T(8,128)(2,1)} %copy-done.4) | copy-start | bytes 196612 | tf_op jit(solution)/shard_map/while/body/eval_jaxpr/cond
  308.4 7.5 %copy-start.2 = (bf16[4,64,128]{2,1,0:T(8,128)(2,1)S(1)}, bf16[4,64,128]{2,1,0:T(8,128)(2,1)}, u32[]{:S(2)}) copy-start(bf16[4,64,128]{2,1,0:T(8,128)(2,1)} %fusion.41) | copy-start | bytes 196612 | tf_op jit(solution)/shard_map/while/body/eval_jaxpr/cond
  316.6 13.3 %collective-permute-start.1 = (bf16[128,2048]{1,0:T(8,128)(2,1)}, bf16[128,2048]{1,0:T(8,128)(2,1)S(1)}, u32[]{:S(2)}, u32[]{:S(2)}) collective-permute-start(bf16[128,2048]{1,0:T(8,128)(2,1)} %get-tuple-element.824), channel_id=1, source_target_pairs={{16,0},{17,1},{18,2},{19,3},{20,4},{21,5},{22,6},{23,7},{24,8},{25... | collective-permute-start | bytes 1572872 | tf_op jit(solution)/shard_map/while/body/eval_jaxpr/ppermute | solution.py:14
  342.9 10.1 %copy-start.3 = (bf16[128,4,64,1]{0,2,3,1:T(8,128)(2,1)}, bf16[128,4,64,1]{0,2,3,1:T(8,128)(2,1)S(1)}, u32[]{:S(2)}) copy-start(bf16[128,4,64,1]{0,2,3,1:T(8,128)(2,1)S(1)} %fusion.73) | copy-start | bytes 196612 | tf_op jit(solution)/shard_map/while/body/eval_jaxpr/cond
  343.3 0.7 copy-start
  344.0 0.6 copy-start.6
  347.5 5.6 %copy-start.1 = (bf16[128,4,4,64]{0,3,2,1:T(8,128)(2,1)S(1)}, bf16[128,4,4,64]{0,3,2,1:T(8,128)(2,1)}, u32[]{:S(2)}) copy-start(bf16[128,4,4,64]{0,3,2,1:T(8,128)(2,1)} %copy-done) | copy-start | bytes 786436 | tf_op jit(solution)/shard_map/while/body/eval_jaxpr/cond
  348.5 6.9 %copy-start.4 = (bf16[128,256]{0,1:T(8,128)(2,1)}, bf16[128,256]{0,1:T(8,128)(2,1)S(1)}, u32[]{:S(2)}) copy-start(bf16[128,256]{0,1:T(8,128)(2,1)S(1)} %copy.59) | copy-start | bytes 196612 | tf_op jit(solution)/shard_map/while/body/eval_jaxpr/cond
  357.9 6.4 %copy-start.5 = (bf16[128,256]{0,1:T(8,128)(2,1)S(1)}, bf16[128,256]{0,1:T(8,128)(2,1)}, u32[]{:S(2)}) copy-start(bf16[128,256]{0,1:T(8,128)(2,1)} %copy-done.4) | copy-start | bytes 196612 | tf_op jit(solution)/shard_map/while/body/eval_jaxpr/cond
  357.9 7.5 %copy-start.2 = (bf16[4,64,128]{2,1,0:T(8,128)(2,1)S(1)}, bf16[4,64,128]{2,1,0:T(8,128)(2,1)}, u32[]{:S(2)}) copy-start(bf16[4,64,128]{2,1,0:T(8,128)(2,1)} %fusion.41) | copy-start | bytes 196612 | tf_op jit(solution)/shard_map/while/body/eval_jaxpr/cond
  366.2 12.3 %collective-permute-start.1 = (bf16[128,2048]{1,0:T(8,128)(2,1)}, bf16[128,2048]{1,0:T(8,128)(2,1)S(1)}, u32[]{:S(2)}, u32[]{:S(2)}) collective-permute-start(bf16[128,2048]{1,0:T(8,128)(2,1)} %get-tuple-element.824), channel_id=1, source_target_pairs={{16,0},{17,1},{18,2},{19,3},{20,4},{21,5},{22,6},{23,7},{24,8},{25... | collective-permute-start | bytes 1572872 | tf_op jit(solution)/shard_map/while/body/eval_jaxpr/ppermute | solution.py:14
  410.7 1.0 copy-start.7
  411.7 119.9 %copy-start.8 = (bf16[1,128]{1,0:T(2,128)(2,1)S(1)}, bf16[1,128]{1,0:T(2,128)(2,1)}, u32[]{:S(2)}) copy-start(bf16[1,128]{1,0:T(2,128)(2,1)} %param.15) | copy-start | bytes 772
Sparse Core Ops, SparseCore 0:
  10.2 53.2 all-gather.7
  65.7 60.3 all-gather.5
  410.9 116.7 reduce-scatter.3
where the time goes:
time: 540 us; the launch traced here: 539 us
  waiting for transfers between devices  314 us (58%)
  matrix products  76.2 us (14%)
  local copies, waits for them, and re-layouts  47.9 us (9%)
  other arithmetic  30.1 us (6%)
  starting transfers between devices  29 us (5%)
  blocking collectives  23.2 us (4%)
  between operations  13.8 us (3%)
    unnamed x4, waiting for transfers between devices  117 us
    ppermute x6, waiting for transfers between devices, shifted(): lax.ppermute(value, axis, [(source, source + steps) for source in range(l...  103 us
    all_gather x1, waiting for transfers between devices, on_device(): lax.all_gather(w_qkv[0], 'fsdp', axis=0, tiled=True)  62.7 us
    dot_general x22, matrix products, mix(): return jnp.einsum(form, left, right, preferred_element_type=jnp.float32)  50.7 us
    all_gather x1, waiting for transfers between devices, on_device(): lax.all_gather(w_out[0], 'fsdp', axis=0, tiled=True)  30.8 us
    ppermute x6, starting transfers between devices, shifted(): lax.ppermute(value, axis, [(source, source + steps) for source in range(l...  28.8 us
    all_gather x1, blocking collectives, on_device(): lax.all_gather(gains[0], 'fsdp', axis=0, tiled=True)  23.2 us
    unnamed x9, local copies, waits for them, and re-layouts  18.5 us
  transfers between devices with their start and end apart: 9, of which 9 were waited for; matrix products, arithmetic and copies ran while one was open for 0% of the time, Pallas kernels for 0%

commit v1 on v0

--- a/solution.py
+++ b/solution.py
@@ -104,7 +104,7 @@
     return (grad_x.astype(jnp.bfloat16), grad_joined)
 
 
-def on_device(inputs, cotangent, gains, w_qkv, w_out):
+def staged(inputs, cotangent, gains, w_qkv, w_out):
     section_count = lax.axis_size("pp")
     section_index = lax.axis_index("pp")
     full_qkv, full_out, full_gain = (
@@ -210,9 +210,60 @@
     return (outputs[None], grad_qkv[None], grad_out[None], grad_gain[None])
 
 
+def pick(first, own, other):
+    return jax.tree.map(lambda left, right: jnp.where(first, left, right), own, other)
+
+
+def two_sections(inputs, cotangent, gains, w_qkv, w_out):
+    first = lax.axis_index("pp") == 0
+    full_gain = lax.all_gather(gains[0], "fsdp", axis=0, tiled=True)
+    full_qkv = lax.all_gather(w_qkv[0], "fsdp", axis=0, tiled=True)
+    full_out = lax.all_gather(w_out[0], "fsdp", axis=0, tiled=True)
+    micro_count, length, width = inputs.shape
+    cosine, sine = rope_tables(length)
+    weights = (full_gain, full_qkv, full_out, cosine, sine)
+    early, sent = [], []
+    for micro in range(micro_count):
+        out, saved = layer_forward(inputs[micro], *weights)
+        early.append((out, saved))
+        sent.append(shifted(out, "pp", 1))
+    late, back = [], []
+    for micro in range(micro_count):
+        out, saved = layer_forward(sent[micro], *weights)
+        grad_x = layer_backward(cotangent[micro], saved, *weights)[0]
+        late.append((out, saved))
+        back.append(shifted(grad_x, "pp", -1))
+    kept = []
+    for micro in range(micro_count):
+        out, saved = pick(first, early[micro], late[micro])
+        grad_in = jnp.where(first, back[micro], cotangent[micro])
+        grad_joined = layer_backward(grad_in, saved, *weights)[1]
+        kept.append((out, saved[2], grad_joined, grad_in, saved[7]))
+    outputs, normed, joined, incoming, context = (jnp.stack(piece) for piece in zip(*kept))
+    return finish(outputs, normed, joined, incoming, context, gains, w_qkv)
+
+
+def finish(outputs, normed, joined, incoming, context, gains, w_qkv):
+    joined_width = joined.shape[-1]
+    summed = lax.psum_scatter(
+        jnp.concatenate(
+            [mix("msd,msj->dj", normed, joined), mix("msd,msc->dc", incoming, context)], axis=1
+        ).astype(jnp.bfloat16),
+        "fsdp",
+        scatter_dimension=0,
+        tiled=True,
+    ).astype(jnp.float32)
+    grad_qkv = summed[:, :joined_width]
+    grad_out = summed[:, joined_width:]
+    grad_gain = jnp.sum(grad_qkv * w_qkv[0].astype(jnp.float32), axis=1) / gains[0].astype(
+        jnp.float32
+    )
+    return (outputs[None], grad_qkv[None], grad_out[None], grad_gain[None])
+
+
 def solution(mesh):
     return jax.shard_map(
-        on_device,
+        two_sections if mesh.shape["pp"] == 2 else staged,
         mesh=mesh,
         in_specs=(
             P(None, "fsdp", None),

time: 540 us -> 429 us (0.79)
  waiting for transfers between devices: 314 us -> 214 us
  matrix products: 76.2 us -> 106 us
  local copies, waits for them, and re-layouts: 47.9 us -> 25.3 us
  starting transfers between devices: 29 us -> 11 us
    ppermute x6 -> x4, waiting for transfers between devices: 103 us -> 19.1 us  [shifted(): lax.ppermute(value, axis, [(source, source + steps) for source in range(l...]
    dot_general x22 -> x30, matrix products: 50.7 us -> 70.9 us  [mix(): return jnp.einsum(form, left, right, preferred_element_type=jnp.float32)]
    ppermute x6 -> x4, starting transfers between devices: 28.8 us -> 10.9 us  [shifted(): lax.ppermute(value, axis, [(source, source + steps) for source in range(l...]
    dynamic_update_slice x6 -> x0, other arithmetic: 8.79 us -> none  [the longest x4 6.35 us: backward_run_layer(): lax.dynamic_update_index_in_dim(buffer, piece, slot_index, 0)]
    all_gather x2, waiting for transfers between devices: 93.4 us -> 84.8 us  [the longest x1 54.9 us: two_sections(): full_qkv = lax.all_gather(w_qkv[0], 'fsdp', axis=0, tiled=True)]
    dynamic_slice x6 -> x0, local copies, waits for them, and re-layouts: 7.66 us -> none  [on_device(): lax.scan(forward_tick, start_carry, jnp.arange(tick_count))]
    unnamed x4, waiting for transfers between devices: 117 us -> 110 us
    dot_general x2 -> x4, matrix products: 5.8 us -> 12.1 us  [layer_backward(): jnp.dot(grad_in, w_out, preferred_element_type=jnp.float32)]
  transfers between devices with their start and end apart: 9 -> 7, of which waited for: 9 -> 6; matrix products, arithmetic and copies ran while one was open for 0% -> 11% of each run, Pallas kernels for 0% -> 0%
where the time goes in v1:
time: 429 us; the launch traced here: 428 us
  waiting for transfers between devices  214 us (50%)
  matrix products  106 us (25%)
  other arithmetic  33.6 us (8%)
  local copies, waits for them, and re-layouts  25.3 us (6%)
  blocking collectives  23.2 us (5%)
  between operations  15 us (3%)
  starting transfers between devices  11 us (3%)
    unnamed x4, waiting for transfers between devices  110 us
    dot_general x30, matrix products, mix(): return jnp.einsum(form, left, right, preferred_element_type=jnp.float32)  70.9 us
    all_gather x1, waiting for transfers between devices, two_sections(): full_qkv = lax.all_gather(w_qkv[0], 'fsdp', axis=0, tiled=True)  54.9 us
    all_gather x1, waiting for transfers between devices, two_sections(): full_out = lax.all_gather(w_out[0], 'fsdp', axis=0, tiled=True)  29.8 us
    all_gather x1, blocking collectives, two_sections(): full_gain = lax.all_gather(gains[0], 'fsdp', axis=0, tiled=True)  23.2 us
    unnamed x139, local copies, waits for them, and re-layouts  20.2 us
    ppermute x4, waiting for transfers between devices, shifted(): lax.ppermute(value, axis, [(source, source + steps) for source in range(l...  19.1 us
    dot_general x4, matrix products, layer_forward(): joined = jnp.dot(normed, w_qkv, preferred_element_type=jnp.float32)  15.2 us
  transfers between devices with their start and end apart: 7, of which 6 were waited for; matrix products, arithmetic and copies ran while one was open for 11% of the time, Pallas kernels for 0%

profile of v1, /device:TPU:0, one launch (start us, length us, event | category | flops | bytes accessed | tf_op | source)
XLA Modules:
  0.0 427.6 jit_solution(14893561579893978954)
XLA Ops:
  8.7 23.2 %all-gather = bf16[1,2048]{1,0:T(2,128)(2,1)S(1)} all-gather(bf16[1,128]{1,0:T(2,128)(2,1)} %param.7), channel_id=2, replica_groups=mesh['pp'=2,'fsdp'=16] {'fsdp'}, dimensions={1}, use_global_device_ids=true | all-gather | bytes 4352 | tf_op jit(solution)/shard_map/all_gather | solution.py:219
  33.6 29.8 %all-gather.8.cloned.1.call-done = bf16[1,2048,1024]{2,1,0:T(8,128)(2,1)} async-done(((bf16[1,128,1024]{2,1,0:T(8,128)(2,1)}), bf16[1,2048,1024]{2,1,0:T(8,128)(2,1)}) %all-gather.8.cloned.1.call-update) | async-done | bytes 4194320 | tf_op jit(solution)/shard_map/all_gather | solution.py:221
  63.5 3.1 fusion.114
  67.4 2.9 fusion.120
  71.2 54.9 %all-gather.6.cloned.1.call-done = bf16[1,2048,1536]{2,1,0:T(8,128)(2,1)} async-done(((bf16[1,128,1536]{2,1,0:T(8,128)(2,1)}), bf16[1,2048,1536]{2,1,0:T(8,128)(2,1)}) %all-gather.6.cloned.1.call-update) | async-done | bytes 6291472 | tf_op jit(solution)/shard_map/all_gather | solution.py:220
  126.1 3.8 fusion.14
  131.3 4.6 %fusion.59 = bf16[128,2048]{1,0:T(8,128)(2,1)} fusion(bf16[128,1024]{0,1:T(8,128)(2,1)S(1)} %bitcast.514, bf16[1,2048,1024]{2,1,0:T(8,128)(2,1)} %all-gather.8.cloned.1.call-done, bf16[2,128,2048]{2,1,0:T(8,128)(2,1)S(1)} %copy-done.1), kind=kOutput, calls=%fused_computation.44 | convolution fusion | flops 537657344 | bytes 5505024 | tf_op jit(solution)/shard_map/sc,dc->sd/dot_general | solution.py:18
  135.9 3.4 collective-permute-start
  139.4 3.8 fusion.10
  145.8 5.4 %collective-permute-done = bf16[128,2048]{1,0:T(8,128)(2,1)S(1)} collective-permute-done((bf16[128,2048]{1,0:T(8,128)(2,1)}, bf16[128,2048]{1,0:T(8,128)(2,1)S(1)}, u32[]{:S(2)}, u32[]{:S(2)}) %collective-permute-start) | collective-permute-done | bytes 524320 | tf_op jit(solution)/shard_map/ppermute | solution.py:14
  151.9 3.8 fusion.12
  159.1 2.1 fusion.185
  161.2 2.1 divide_convert_fusion.2
  163.2 2.0 fusion.94
  165.8 2.4 broadcast_multiply_fusion.3
  168.1 2.4 fusion.113
  170.6 1.6 convolution_convert_fusion.1
  172.9 3.7 fusion.53
  176.7 4.6 %collective-permute-start.1 = (bf16[128,2048]{1,0:T(8,128)(2,1)S(1)}, bf16[128,2048]{1,0:T(8,128)(2,1)S(1)}, u32[]{:S(2)}, u32[]{:S(2)}) collective-permute-start(bf16[128,2048]{1,0:T(8,128)(2,1)S(1)} %fusion.53), channel_id=1, source_target_pairs={{0,16},{1,17},{2,18},{3,19},{4,20},{5,21},{6,22},{7,23},{8,24},{9,... | collective-permute-start | bytes 1572872 | tf_op jit(solution)/shard_map/ppermute | solution.py:14
  181.3 2.5 fusion.130
  183.9 2.7 broadcast_select_fusion.3
  188.0 3.9 collective-permute-done.1
  192.6 3.8 fusion.8
  201.1 2.4 fusion.107
  203.6 2.3 broadcast_multiply_fusion.1
  205.9 2.5 broadcast_select_fusion
  211.3 3.2 fusion.147
  215.1 1.9 fusion.132
  217.2 5.2 %fusion.155 = (f32[128]{0:T(128)S(1)}, f32[128,2048]{1,0:T(8,128)S(1)}) fusion(bf16[128,2048]{1,0:T(8,128)(2,1)S(1)} %collective-permute-done.1, f32[2048]{0:T(1024)S(1)} %bitcast.499, bf16[1,2048,1536]{2,1,0:T(8,128)(2,1)} %all-gather.6.cloned.1.call-done, bf16[128,256]{0,1:T(8,128)(2,1)S(1)} %bitcast.516, bf16[128,256]{0,1:T(8,128)(2,1)S(1)} %bitcast.501, ...), kind=kOutput, calls=%fused_computation.158 | convolution fusion | flops 807534464 | bytes 8266240 | tf_op jit(solution)/shard_map/sj,dj->sd/dot_general | solution.py:18
  222.5 1.6 fusion.146
  225.4 2.8 broadcast_select_fusion.2
  228.1 1.6 collective-permute-start.2
  231.4 9.8 %collective-permute-done.3 = bf16[128,2048]{1,0:T(8,128)(2,1)} collective-permute-done((bf16[128,2048]{1,0:T(8,128)(2,1)}, bf16[128,2048]{1,0:T(8,128)(2,1)}, u32[]{:S(2)}, u32[]{:S(2)}) %collective-permute-start.3) | collective-permute-done | bytes 524320 | tf_op jit(solution)/shard_map/ppermute | solution.py:14
  241.2 3.1 fusion.123
  245.8 3.0 fusion.129
  248.8 2.3 fusion.104
  251.1 2.0 fusion.133
  253.1 3.1 fusion.117
  256.4 2.0 fusion.131
  258.4 2.2 convolution_bitcast_fusion.2
  260.5 3.1 fusion.110
  263.6 3.1 broadcast_multiply_fusion.2
  271.1 2.3 bitcast_convert_fusion
  273.3 12.6 %pad_maximum_fusion = bf16[2048,2560]{0,1:T(8,128)(2,1)} fusion(bf16[2048,1024]{0,1:T(8,128)(2,1)S(1)} %bitcast_convert_fusion.1, bf16[2048,1536]{0,1:T(8,128)(2,1)S(1)} %bitcast_convert_fusion), kind=kLoop, calls=%fused_computation.5 | loop fusion | flops 20971520 | bytes 20971520 | tf_op jit(solution)/shard_map/concatenate | solution.py:249
  285.9 13.8 %copy.184 = bf16[2048,2560]{1,0:T(8,128)(2,1)} copy(bf16[2048,2560]{0,1:T(8,128)(2,1)} %pad_maximum_fusion) | data formatting | bytes 20971520
  301.0 4.4 %fusion.65 = bf16[1,128,2048]{2,1,0:T(8,128)(2,1)S(1)} fusion(bf16[128,2048]{1,0:T(8,128)(2,1)} %fusion.59, bf16[128,1024]{0,1:T(8,128)(2,1)S(1)} %bitcast.503, bf16[1,2048,1024]{2,1,0:T(8,128)(2,1)} %all-gather.8.cloned.1.call-done, bf16[128,2048]{1,0:T(8,128)(2,1)S(1)} %collective-permute-done, pred[]{:T(512)S(6)} %eq.3), kind=kOutput, calls=%fused_computation.46 | convolution fusion | flops 537919488 | bytes 6029313 | tf_op jit(solution)/shard_map/sc,dc->sd/dot_general | solution.py:18
  305.4 1.6 fusion.71
  308.1 108.5 %reduce-scatter.4.cloned.1.call-done = bf16[128,2560]{1,0:T(8,128)(2,1)} async-done(((bf16[2048,2560]{1,0:T(8,128)(2,1)}), bf16[128,2560]{1,0:T(8,128)(2,1)}) %reduce-scatter.4.cloned.1.call-update) | async-done | bytes 655376
  (235 shorter events, 39.6 us)
Async XLA Ops:
  7.2 60.3 %copy-start.3 = (bf16[2,128,2048]{2,1,0:T(8,128)(2,1)S(1)}, bf16[2,128,2048]{2,1,0:T(8,128)(2,1)}, u32[]{:S(2)}) copy-start(bf16[2,128,2048]{2,1,0:T(8,128)(2,1)} %param.6) | copy-start | bytes 3145732
  7.2 56.3 %all-gather.8.cloned.1.call-start = ((), (), s32[]{:S(2)}) async-start(), calls=%async_computation.2 | async-start | bytes 4456448 | tf_op jit(solution)/shard_map/all_gather | solution.py:221
  7.9 118.2 %all-gather.6.cloned.1.call-start = ((), (), s32[]{:S(2)}) async-start(), calls=%async_computation.1 | async-start | bytes 6684672 | tf_op jit(solution)/shard_map/all_gather | solution.py:220
  8.7 408.0 %reduce-scatter.4.cloned.1.call-start = ((), (), s32[]{:S(2)}) async-start(), calls=%async_computation.3 | async-start | bytes 11141120
  31.9 98.7 %copy-start.41 = (pred[128,128]{0,1:T(8,128)(4,1)}, pred[128,128]{0,1:T(8,128)(4,1)S(1)}, u32[]{:S(2)}) copy-start(pred[128,128]{0,1:T(8,128)(4,1)S(1)} %iota_compare_fusion) | copy-start | bytes 49156
  33.6 105.7 %copy-start.56 = (f32[128]{0:T(128)}, f32[128]{0:T(128)S(1)}, u32[]{:S(2)}) copy-start(f32[128]{0:T(128)S(1)} %add_rsqrt_fusion.1) | copy-start | bytes 1540
  33.6 92.5 %copy-start.58 = (f32[128]{0:T(128)}, f32[128]{0:T(128)S(1)}, u32[]{:S(2)}) copy-start(f32[128]{0:T(128)S(1)} %add_rsqrt_fusion.3) | copy-start | bytes 1540
  66.5 59.6 %copy-start.1 = (bf16[2,128,2048]{2,1,0:T(8,128)(2,1)S(1)}, bf16[2,128,2048]{2,1,0:T(8,128)(2,1)}, u32[]{:S(2)}) copy-start(bf16[2,128,2048]{2,1,0:T(8,128)(2,1)} %param.5) | copy-start | bytes 3145732
  130.6 5.3 %copy-start.27 = (bf16[128,4,4,64]{0,3,2,1:T(8,128)(2,1)}, bf16[128,4,4,64]{0,3,2,1:T(8,128)(2,1)S(1)}, u32[]{:S(2)}) copy-start(bf16[128,4,4,64]{0,3,2,1:T(8,128)(2,1)S(1)} %fusion.183) | copy-start | bytes 786436
  131.3 4.6 %copy-start.39 = (bf16[4,64,4,128]{3,1,2,0:T(8,128)(2,1)}, bf16[4,64,4,128]{3,1,2,0:T(8,128)(2,1)S(1)}, u32[]{:S(2)}) copy-start(bf16[4,64,4,128]{3,1,2,0:T(8,128)(2,1)S(1)} %convolution_convert_fusion.3) | copy-start | bytes 786436
  135.9 15.3 %collective-permute-start = (bf16[128,2048]{1,0:T(8,128)(2,1)}, bf16[128,2048]{1,0:T(8,128)(2,1)S(1)}, u32[]{:S(2)}, u32[]{:S(2)}) collective-permute-start(bf16[128,2048]{1,0:T(8,128)(2,1)} %fusion.59), channel_id=1, source_target_pairs={{0,16},{1,17},{2,18},{3,19},{4,20},{5,21},{6,22},{7,23},{8,24},{9,... | collective-permute-start | bytes 1572872 | tf_op jit(solution)/shard_map/ppermute | solution.py:14
  159.1 4.2 copy-start.29
  159.1 6.3 %copy-start.13 = (bf16[128,1024]{0,1:T(8,128)(2,1)S(1)}, bf16[128,1024]{0,1:T(8,128)(2,1)}, u32[]{:S(2)}) copy-start(bf16[128,1024]{0,1:T(8,128)(2,1)} %copy.129) | copy-start | bytes 786436
  161.1 7.0 %copy-start.17 = (bf16[128,4,4,64]{0,3,2,1:T(8,128)(2,1)}, bf16[128,4,4,64]{0,3,2,1:T(8,128)(2,1)S(1)}, u32[]{:S(2)}) copy-start(bf16[128,4,4,64]{0,3,2,1:T(8,128)(2,1)S(1)} %get-tuple-element.60) | copy-start | bytes 786436
  161.1 4.2 copy-start.26
  161.1 9.4 %copy-start.34 = (bf16[128,256]{0,1:T(8,128)(2,1)S(1)}, bf16[128,256]{0,1:T(8,128)(2,1)}, u32[]{:S(2)}) copy-start(bf16[128,256]{0,1:T(8,128)(2,1)} %copy.119) | copy-start | bytes 196612
  161.1 9.4 %copy-start.52 = (bf16[128,4,64]{0,2,1:T(8,128)(2,1)S(1)}, bf16[128,4,64]{0,2,1:T(8,128)(2,1)}, u32[]{:S(2)}) copy-start(bf16[128,4,64]{0,2,1:T(8,128)(2,1)} %get-tuple-element.59) | copy-start | bytes 196612
  176.6 9.9 %copy-start.6 = (bf16[128,2048]{1,0:T(8,128)(2,1)}, bf16[128,2048]{1,0:T(8,128)(2,1)S(1)}, u32[]{:S(2)}) copy-start(bf16[128,2048]{1,0:T(8,128)(2,1)S(1)} %fusion.53) | copy-start | bytes 1572868
  176.6 7.2 %copy-start.44 = (f32[128,4,64]{0,2,1:T(8,128)S(1)}, f32[128,4,64]{0,2,1:T(8,128)}, u32[]{:S(2)}) copy-start(f32[128,4,64]{0,2,1:T(8,128)} %get-tuple-element.82) | copy-start | bytes 393220
  176.6 7.2 %copy-start.40 = (bf16[4,64,4,128]{3,1,2,0:T(8,128)(2,1)S(1)}, bf16[4,64,4,128]{3,1,2,0:T(8,128)(2,1)}, u32[]{:S(2)}) copy-start(bf16[4,64,4,128]{3,1,2,0:T(8,128)(2,1)} %copy-done.39) | copy-start | bytes 786436
  176.6 9.9 %copy-start.28 = (bf16[128,4,4,64]{0,3,2,1:T(8,128)(2,1)S(1)}, bf16[128,4,4,64]{0,3,2,1:T(8,128)(2,1)}, u32[]{:S(2)}) copy-start(bf16[128,4,4,64]{0,3,2,1:T(8,128)(2,1)} %copy-done.27) | copy-start | bytes 786436
  176.6 9.9 %copy-start.42 = (pred[128,128]{0,1:T(8,128)(4,1)S(1)}, pred[128,128]{0,1:T(8,128)(4,1)}, u32[]{:S(2)}) copy-start(pred[128,128]{0,1:T(8,128)(4,1)} %copy-done.41) | copy-start | bytes 49156
  176.7 9.9 %copy-start.51 = (bf16[128,4,64]{0,2,1:T(8,128)(2,1)S(1)}, bf16[128,4,64]{0,2,1:T(8,128)(2,1)}, u32[]{:S(2)}) copy-start(bf16[128,4,64]{0,2,1:T(8,128)(2,1)} %copy-done.50) | copy-start | bytes 196612
  176.7 9.9 %copy-start.64 = (bf16[4,4,128,128]{2,3,1,0:T(8,128)(2,1)S(1)}, bf16[4,4,128,128]{2,3,1,0:T(8,128)(2,1)}, u32[]{:S(2)}) copy-start(bf16[4,4,128,128]{2,3,1,0:T(8,128)(2,1)} %divide_convert_fusion.2) | copy-start | bytes 1572868
  176.7 15.2 %collective-permute-start.1 = (bf16[128,2048]{1,0:T(8,128)(2,1)S(1)}, bf16[128,2048]{1,0:T(8,128)(2,1)S(1)}, u32[]{:S(2)}, u32[]{:S(2)}) collective-permute-start(bf16[128,2048]{1,0:T(8,128)(2,1)S(1)} %fusion.53), channel_id=1, source_target_pairs={{0,16},{1,17},{2,18},{3,19},{4,20},{5,21},{6,22},{7,23},{8,24},{9,... | collective-permute-start | bytes 1572872 | tf_op jit(solution)/shard_map/ppermute | solution.py:14
  197.0 6.6 %copy-start.14 = (bf16[128,4,4,64]{0,3,2,1:T(8,128)(2,1)}, bf16[128,4,4,64]{0,3,2,1:T(8,128)(2,1)S(1)}, u32[]{:S(2)}) copy-start(bf16[128,4,4,64]{0,3,2,1:T(8,128)(2,1)S(1)} %fusion.189) | copy-start | bytes 786436
  198.0 5.6 %copy-start.30 = (bf16[128,4,64]{0,2,1:T(8,128)(2,1)}, bf16[128,4,64]{0,2,1:T(8,128)(2,1)S(1)}, u32[]{:S(2)}) copy-start(bf16[128,4,64]{0,2,1:T(8,128)(2,1)S(1)} %get-tuple-element.75) | copy-start | bytes 196612
  205.9 5.0 %slice-start = ((s8[6291456]{0:T(1024)(128)(4,1)}), s8[2097152]{0:T(1024)(128)(4,1)S(1)}, s32[]{:S(2)}) async-start(s8[6291456]{0:T(1024)(128)(4,1)} %bitcast.454), calls=%async_computation.4 | async-start | bytes 4194304
  217.1 5.3 %copy-start.4 = (bf16[2,128,2048]{2,1,0:T(8,128)(2,1)S(1)}, bf16[2,128,2048]{2,1,0:T(8,128)(2,1)}, u32[]{:S(2)}) copy-start(bf16[2,128,2048]{2,1,0:T(8,128)(2,1)} %param.6) | copy-start | bytes 3145732
  217.1 5.3 %copy-start.5 = (f32[128,2048]{1,0:T(8,128)S(1)}, f32[128,2048]{1,0:T(8,128)}, u32[]{:S(2)}) copy-start(f32[128,2048]{1,0:T(8,128)} %get-tuple-element.85) | copy-start | bytes 3145732
  217.1 5.3 %copy-start.61 = (f32[128]{0:T(128)S(1)}, f32[128]{0:T(128)}, u32[]{:S(2)}) copy-start(f32[128]{0:T(128)} %get-tuple-element.76) | copy-start | bytes 1540
  217.1 5.3 %copy-start.62 = (f32[128]{0:T(128)S(1)}, f32[128]{0:T(128)}, u32[]{:S(2)}) copy-start(f32[128]{0:T(128)} %get-tuple-element.78) | copy-start | bytes 1540
  217.2 5.3 %copy-start.63 = (f32[128]{0:T(128)S(1)}, f32[128]{0:T(128)}, u32[]{:S(2)}) copy-start(f32[128]{0:T(128)} %broadcast_multiply_fusion.5) | copy-start | bytes 1540
  222.4 7.4 %copy-start.2 = (bf16[2,128,2048]{2,1,0:T(8,128)(2,1)S(1)}, bf16[2,128,2048]{2,1,0:T(8,128)(2,1)}, u32[]{:S(2)}) copy-start(bf16[2,128,2048]{2,1,0:T(8,128)(2,1)} %param.5) | copy-start | bytes 3145732
  222.4 7.4 %copy-start.57 = (f32[128]{0:T(128)S(1)}, f32[128]{0:T(128)}, u32[]{:S(2)}) copy-start(f32[128]{0:T(128)} %copy-done.56) | copy-start | bytes 1540
  222.4 7.4 %copy-start.59 = (f32[128]{0:T(128)S(1)}, f32[128]{0:T(128)}, u32[]{:S(2)}) copy-start(f32[128]{0:T(128)} %copy-done.58) | copy-start | bytes 1540
  224.1 17.1 %collective-permute-start.3 = (bf16[128,2048]{1,0:T(8,128)(2,1)}, bf16[128,2048]{1,0:T(8,128)(2,1)}, u32[]{:S(2)}, u32[]{:S(2)}) collective-permute-start(bf16[128,2048]{1,0:T(8,128)(2,1)} %get-tuple-element.25), channel_id=1, source_target_pairs={{16,0},{17,1},{18,2},{19,3},{20,4},{21,5},{22,6},{23,7},{24,8},{25... | collective-permute-start | bytes 1572872 | tf_op jit(solution)/shard_map/ppermute | solution.py:14
  228.1 16.3 %copy-start.35 = (bf16[128,256]{0,1:T(8,128)(2,1)S(1)}, bf16[128,256]{0,1:T(8,128)(2,1)}, u32[]{:S(2)}) copy-start(bf16[128,256]{0,1:T(8,128)(2,1)} %copy.119) | copy-start | bytes 196612
  228.1 24.9 %collective-permute-start.2 = (bf16[128,2048]{1,0:T(8,128)(2,1)}, bf16[128,2048]{1,0:T(8,128)(2,1)}, u32[]{:S(2)}, u32[]{:S(2)}) collective-permute-start(bf16[128,2048]{1,0:T(8,128)(2,1)} %get-tuple-element.24), channel_id=1, source_target_pairs={{16,0},{17,1},{18,2},{19,3},{20,4},{21,5},{22,6},{23,7},{24,8},{25... | collective-permute-start | bytes 1572872 | tf_op jit(solution)/shard_map/ppermute | solution.py:14
  231.4 14.4 %copy-start.15 = (bf16[128,4,4,64]{0,3,2,1:T(8,128)(2,1)S(1)}, bf16[128,4,4,64]{0,3,2,1:T(8,128)(2,1)}, u32[]{:S(2)}) copy-start(bf16[128,4,4,64]{0,3,2,1:T(8,128)(2,1)} %copy-done.14) | copy-start | bytes 786436
  231.4 14.4 %copy-start.32 = (bf16[128,4,4,64]{0,3,2,1:T(8,128)(2,1)S(1)}, bf16[128,4,4,64]{0,3,2,1:T(8,128)(2,1)}, u32[]{:S(2)}) copy-start(bf16[128,4,4,64]{0,3,2,1:T(8,128)(2,1)} %get-tuple-element.61) | copy-start | bytes 786436
  231.4 17.4 %copy-start.31 = (bf16[128,4,64]{0,2,1:T(8,128)(2,1)S(1)}, bf16[128,4,64]{0,2,1:T(8,128)(2,1)}, u32[]{:S(2)}) copy-start(bf16[128,4,64]{0,2,1:T(8,128)(2,1)} %copy-done.30) | copy-start | bytes 196612
  231.4 17.4 %copy-start.53 = (bf16[128,4,64]{0,2,1:T(8,128)(2,1)S(1)}, bf16[128,4,64]{0,2,1:T(8,128)(2,1)}, u32[]{:S(2)}) copy-start(bf16[128,4,64]{0,2,1:T(8,128)(2,1)} %get-tuple-element.59) | copy-start | bytes 196612
  253.1 10.5 %copy-start.18 = (bf16[128,4,4,64]{0,3,2,1:T(8,128)(2,1)S(1)}, bf16[128,4,4,64]{0,3,2,1:T(8,128)(2,1)}, u32[]{:S(2)}) copy-start(bf16[128,4,4,64]{0,3,2,1:T(8,128)(2,1)} %copy-done.17) | copy-start | bytes 786436
  300.7 4.7 %copy-start.7 = (bf16[128,2048]{1,0:T(8,128)(2,1)S(1)}, bf16[128,2048]{1,0:T(8,128)(2,1)}, u32[]{:S(2)}) copy-start(bf16[128,2048]{1,0:T(8,128)(2,1)} %copy-done.6) | copy-start | bytes 1572868
  300.7 4.7 %copy-start.25 = (bf16[4,64,4,128]{3,1,2,0:T(8,128)(2,1)S(1)}, bf16[4,64,4,128]{3,1,2,0:T(8,128)(2,1)}, u32[]{:S(2)}) copy-start(bf16[4,64,4,128]{3,1,2,0:T(8,128)(2,1)} %get-tuple-element.91) | copy-start | bytes 786436
  300.9 4.5 %copy-start = (bf16[1,2048,1024]{2,1,0:T(8,128)(2,1)S(1)}, bf16[1,2048,1024]{2,1,0:T(8,128)(2,1)}, u32[]{:S(2)}) copy-start(bf16[1,2048,1024]{2,1,0:T(8,128)(2,1)} %all-gather.8.cloned.1.call-done) | copy-start | bytes 12582916
  308.1 112.5 %copy-start.60 = (bf16[1,128]{1,0:T(2,128)(2,1)S(1)}, bf16[1,128]{1,0:T(2,128)(2,1)}, u32[]{:S(2)}) copy-start(bf16[1,128]{1,0:T(2,128)(2,1)} %param.7) | copy-start | bytes 772
  (26 other events, 48.3 us)
Sparse Core Ops, SparseCore 0:
  10.2 53.2 all-gather.7
  65.8 60.3 all-gather.5
  299.9 116.7 reduce-scatter.3

commit v2 on v1

--- a/solution.py
+++ b/solution.py
@@ -1,11 +1,16 @@
+import functools
+
 import jax
 import jax.numpy as jnp
 from jax import lax
+from jax.experimental import pallas as pl
+from jax.experimental.pallas import tpu as pltpu
 from jax.sharding import PartitionSpec as P
 
 HEADS = 16
 KV_HEADS = 4
 HEAD_DIM = 64
+MESH = pl.DeviceIdType.MESH
 
 
 def shifted(value, axis, steps):
@@ -210,15 +215,235 @@
     return (outputs[None], grad_qkv[None], grad_out[None], grad_gain[None])
 
 
+def place(count):
+    me = lax.axis_index("fsdp")
+    return (count // 4, me // 4, (me // 2) % 2, me % 2)
+
+
+def at(outer, side, core):
+    return (outer * 2 + side) * 2 + core
+
+
+def remote(source, target, send_sem, recv_sem, device):
+    return pltpu.make_async_remote_copy(
+        src_ref=source,
+        dst_ref=target,
+        send_sem=send_sem,
+        recv_sem=recv_sem,
+        device_id={"fsdp": device},
+        device_id_type=MESH,
+    )
+
+
+def greet(outers, outer, side, core):
+    barrier = pltpu.get_barrier_semaphore()
+    peers = [at((outer + step) % outers, side, core) for step in range(1, outers)]
+    peers += [at(outer, 1 - side, core), at(outer, side, 1 - core)]
+    for peer in peers:
+        pl.semaphore_signal(barrier, inc=1, device_id={"fsdp": peer}, device_id_type=MESH)
+    pl.semaphore_wait(barrier, len(peers))
+
+
+def gather_kernel(
+    count, qkv, out, gain, full_qkv, full_out, full_gain, own, z_out, z_in, x_out, x_in, c_out, c_in
+):
+    outers, outer, side, core = place(count)
+    greet(outers, outer, side, core)
+    parts = [(gain, full_gain, 0, gain.shape[0])]
+    for source, target in ((qkv, full_qkv), (out, full_out)):
+        half = source.shape[0] // 2
+        parts += [(source, target, 0, half), (source, target, half, half)]
+    beside, partner = at(outer, 1 - side, core), at(outer, side, 1 - core)
+
+    def rows(part, owner):
+        source, target, start, size = part
+        first = pl.multiple_of(owner * source.shape[0] + start, 16)
+        return target.at[pl.ds(first, size)]
+
+    started, local = [], []
+
+    def send(source, target, send_sem, recv_sem, device):
+        copy = remote(source, target, send_sem, recv_sem, device)
+        copy.start()
+        started.append(copy)
+
+    for j, part in enumerate(parts):
+        source, target, start, size = part
+        block, spot = source.at[pl.ds(start, size)], rows(part, at(outer, side, core))
+        for step in range(1, outers):
+            peer = at((outer + step) % outers, side, core)
+            send(block, spot, z_out.at[step, j], z_in.at[step, j], peer)
+        send(block, spot, x_out.at[0, j], x_in.at[0, j], beside)
+        send(block, spot, c_out.at[0, 0, j], c_in.at[0, 0, j], partner)
+        copy = pltpu.make_async_copy(block, spot, own.at[j])
+        copy.start()
+        local.append(copy)
+    for j, part in enumerate(parts):
+        for step in range(1, outers):
+            spot = rows(part, at((outer + outers - step) % outers, side, core))
+            remote(spot, spot, z_out.at[step, j], z_in.at[step, j], beside).wait_recv()
+            send(spot, spot, x_out.at[step, j], x_in.at[step, j], beside)
+            send(spot, spot, c_out.at[0, step, j], c_in.at[0, step, j], partner)
+        for step in range(outers):
+            spot = rows(part, at((outer + outers - step) % outers, 1 - side, core))
+            remote(spot, spot, x_out.at[step, j], x_in.at[step, j], beside).wait_recv()
+            send(spot, spot, c_out.at[1, step, j], c_in.at[1, step, j], partner)
+    for j, part in enumerate(parts):
+        for over in range(2):
+            for step in range(outers):
+                origin = at(
+                    (outer + outers - step) % outers, 1 - side if over else side, 1 - core
+                )
+                spot = rows(part, origin)
+                remote(
+                    spot, spot, c_out.at[over, step, j], c_in.at[over, step, j], partner
+                ).wait_recv()
+    for copy in started:
+        copy.wait_send()
+    for copy in local:
+        copy.wait()
+
+
+def gather(qkv, out, gain):
+    count = lax.axis_size("fsdp")
+    outers = count // 4
+    gain = jnp.broadcast_to(gain[None], (16, gain.shape[0]))
+    sems = [(outers, 5), (outers, 5), (outers, 5), (outers, 5), (2, outers, 5), (2, outers, 5)]
+    full_qkv, full_out, full_gain = pl.pallas_call(
+        functools.partial(gather_kernel, count),
+        out_shape=[
+            jax.ShapeDtypeStruct((count * block.shape[0], block.shape[1]), block.dtype)
+            for block in (qkv, out, gain)
+        ],
+        in_specs=[pl.BlockSpec(memory_space=pl.ANY)] * 3,
+        out_specs=[pl.BlockSpec(memory_space=pl.ANY)] * 3,
+        scratch_shapes=[pltpu.SemaphoreType.DMA((5,))]
+        + [pltpu.SemaphoreType.DMA(shape) for shape in sems],
+        compiler_params=pltpu.CompilerParams(collective_id=0, has_side_effects=True),
+    )(qkv, out, gain)
+    return (full_qkv, full_out, full_gain.reshape(count, 16, -1)[:, 0].reshape(-1))
+
+
+def reduce_kernel(
+    count, normed, joined, incoming, context, sum_qkv, sum_out,
+    c_buf, own, c_got, x_buf, x_got, z_buf, z_got, c_out, c_in, x_out, x_in, z_out, z_in,
+):
+    outers, outer, side, core = place(count)
+    depth, width = sum_qkv.shape
+    beside, partner = at(outer, 1 - side, core), at(outer, side, 1 - core)
+    greet(outers, outer, side, core)
+
+    def term(index, target):
+        columns = pl.ds(pl.multiple_of(index * depth, depth), depth)
+        form = (((0,), (0,)), ((), ()))
+        target[:, :width] = lax.dot_general(
+            normed[:, columns], joined[...], form, preferred_element_type=jnp.float32
+        ).astype(jnp.bfloat16)
+        target[:, width:] = lax.dot_general(
+            incoming[:, columns], context[...], form, preferred_element_type=jnp.float32
+        ).astype(jnp.bfloat16)
+
+    def to_core(k):
+        return remote(c_buf.at[k], c_got.at[k], c_out.at[k], c_in.at[k], partner)
+
+    def to_side(k):
+        return remote(x_buf.at[k], x_got.at[k], x_out.at[k], x_in.at[k], beside)
+
+    def to_outer(k):
+        peer = at((outer + k + 1) % outers, side, core)
+        return remote(z_buf.at[k], z_got.at[k], z_out.at[k], z_in.at[k], peer)
+
+    def wide(ref):
+        return ref[...].astype(jnp.float32)
+
+    def combine(k):
+        to_core(k).wait_recv()
+        both = (wide(own.at[k]) + wide(c_got.at[k])).astype(jnp.bfloat16)
+
+        @pl.when(k < outers)
+        def _():
+            x_buf[k % outers] = both
+            to_side(k % outers).start()
+
+        @pl.when(k >= outers)
+        def _():
+            own[k] = both
+
+    def one(k, carry):
+        where = (outer + k + 1) % outers
+        over = k // outers
+        there = over * side + (1 - over) * (1 - side)
+        term(at(where, there, 1 - core), c_buf.at[k])
+        to_core(k).start()
+        term(at(where, there, core), own.at[k])
+
+        @pl.when(k > 0)
+        def _():
+            combine(k - 1)
+
+        return carry
+
+    lax.fori_loop(0, 2 * outers, one, 0)
+    combine(2 * outers - 1)
+
+    def two(k, carry):
+        to_side(k).wait_recv()
+        z_buf[k] = (wide(own.at[outers + k]) + wide(x_got.at[k])).astype(jnp.bfloat16)
+        to_outer(k).start()
+        return carry
+
+    lax.fori_loop(0, outers - 1, two, 0)
+    last = outers - 1
+    to_side(last).wait_recv()
+    total = wide(own.at[outers + last]) + wide(x_got.at[last])
+    for k in range(last):
+        to_outer(k).wait_recv()
+        total += wide(z_got.at[k])
+    sum_qkv[...] = total[:, :width]
+    sum_out[...] = total[:, width:]
+
+    for k in range(2 * outers):
+        to_core(k).wait_send()
+    for k in range(outers):
+        to_side(k).wait_send()
+    for k in range(last):
+        to_outer(k).wait_send()
+
+
+def reduce_terms(normed, joined, incoming, context):
+    count = lax.axis_size("fsdp")
+    outers = count // 4
+    tokens, width = normed.shape
+    depth = width // count
+    columns = joined.shape[1] + context.shape[1]
+
+    def slots(number):
+        return pltpu.VMEM((number, depth, columns), jnp.bfloat16)
+
+    numbers = (2 * outers, 2 * outers, 2 * outers, outers, outers, outers - 1, outers - 1)
+    sems = (2 * outers, 2 * outers, outers, outers, outers - 1, outers - 1)
+    return pl.pallas_call(
+        functools.partial(reduce_kernel, count),
+        out_shape=[
+            jax.ShapeDtypeStruct((depth, piece.shape[1]), jnp.float32) for piece in (joined, context)
+        ],
+        in_specs=[pl.BlockSpec(memory_space=pltpu.VMEM)] * 4,
+        out_specs=[pl.BlockSpec(memory_space=pltpu.VMEM)] * 2,
+        scratch_shapes=[slots(number) for number in numbers]
+        + [pltpu.SemaphoreType.DMA((number,)) for number in sems],
+        compiler_params=pltpu.CompilerParams(
+            collective_id=1, has_side_effects=True, vmem_limit_bytes=48 * 1024 * 1024
+        ),
+    )(normed, joined, incoming, context)
+
+
 def pick(first, own, other):
     return jax.tree.map(lambda left, right: jnp.where(first, left, right), own, other)
 
 
 def two_sections(inputs, cotangent, gains, w_qkv, w_out):
     first = lax.axis_index("pp") == 0
-    full_gain = lax.all_gather(gains[0], "fsdp", axis=0, tiled=True)
-    full_qkv = lax.all_gather(w_qkv[0], "fsdp", axis=0, tiled=True)
-    full_out = lax.all_gather(w_out[0], "fsdp", axis=0, tiled=True)
+    full_qkv, full_out, full_gain = gather(w_qkv[0], w_out[0], gains[0])
     micro_count, length, width = inputs.shape
     cosine, sine = rope_tables(length)
     weights = (full_gain, full_qkv, full_out, cosine, sine)
@@ -239,26 +464,17 @@
         grad_in = jnp.where(first, back[micro], cotangent[micro])
         grad_joined = layer_backward(grad_in, saved, *weights)[1]
         kept.append((out, saved[2], grad_joined, grad_in, saved[7]))
-    outputs, normed, joined, incoming, context = (jnp.stack(piece) for piece in zip(*kept))
+    outputs, normed, joined, incoming, context = zip(*kept)
     return finish(outputs, normed, joined, incoming, context, gains, w_qkv)
 
 
 def finish(outputs, normed, joined, incoming, context, gains, w_qkv):
-    joined_width = joined.shape[-1]
-    summed = lax.psum_scatter(
-        jnp.concatenate(
-            [mix("msd,msj->dj", normed, joined), mix("msd,msc->dc", incoming, context)], axis=1
-        ).astype(jnp.bfloat16),
-        "fsdp",
-        scatter_dimension=0,
-        tiled=True,
-    ).astype(jnp.float32)
-    grad_qkv = summed[:, :joined_width]
-    grad_out = summed[:, joined_width:]
+    pieces = (jnp.concatenate(piece, axis=0) for piece in (normed, joined, incoming, context))
+    grad_qkv, grad_out = reduce_terms(*pieces)
     grad_gain = jnp.sum(grad_qkv * w_qkv[0].astype(jnp.float32), axis=1) / gains[0].astype(
         jnp.float32
     )
-    return (outputs[None], grad_qkv[None], grad_out[None], grad_gain[None])
+    return (jnp.stack(outputs)[None], grad_qkv[None], grad_out[None], grad_gain[None])
 
 
 def solution(mesh):

time: 429 us -> 335 us (0.78)
  waiting for transfers between devices: 214 us -> 21.3 us
  Pallas kernels: 0 us -> 161 us
  blocking collectives: 23.2 us -> 0 us
  matrix products: 106 us -> 86.1 us
  between operations: 15 us -> 1.87 us
    pallas_call x0 -> x2, Pallas kernels: none -> 161 us  [the longest x1 83 us: reduce_terms(): pl.pallas_call(functools.partial(reduce_kernel, count), out_shape=[jax.Sh...]
    unnamed x4 -> x0, waiting for transfers between devices: 110 us -> none
    all_gather x2 -> x0, waiting for transfers between devices: 84.8 us -> none  [the longest x1 54.9 us: two_sections(): full_qkv = lax.all_gather(w_qkv[0], 'fsdp', axis=0, tiled=True)]
    all_gather x1 -> x0, blocking collectives: 23.2 us -> none  [two_sections(): full_gain = lax.all_gather(gains[0], 'fsdp', axis=0, tiled=True)]
    unnamed x139 -> x116, local copies, waits for them, and re-layouts: 20.2 us -> 3.83 us
    dot_general x30 -> x28, matrix products: 70.9 us -> 54.8 us  [mix(): return jnp.einsum(form, left, right, preferred_element_type=jnp.float32)]
    concatenate x1 -> x4, other arithmetic: 12.6 us -> 0.24 us  [finish(): jnp.concatenate(piece, axis=0)]
    reshape x0 -> x6, local copies, waits for them, and re-layouts: none -> 6.62 us  [the longest x2 4.1 us: layer_backward(): mix('kgst,tkh->skgh', grad_scores, keys).reshape(length, HEADS, HEAD_DIM)]
  transfers between devices with their start and end apart: 7 -> 4, of which waited for: 6 -> 3; matrix products, arithmetic and copies ran while one was open for 11% -> 10% of each run, Pallas kernels for 0% -> 0%
where the time goes in v2:
time: 335 us; the launch traced here: 334 us
  Pallas kernels  161 us (48%)
  matrix products  86.1 us (26%)
  other arithmetic  30.9 us (9%)
  local copies, waits for them, and re-layouts  24.1 us (7%)
  waiting for transfers between devices  21.3 us (6%)
  starting transfers between devices  8.46 us (3%)
    pallas_call x1, Pallas kernels, reduce_terms(): pl.pallas_call(functools.partial(reduce_kernel, count), out_shape=[jax.Sh...  83 us
    pallas_call x1, Pallas kernels, gather(): pl.pallas_call(functools.partial(gather_kernel, count), out_shape=[jax.Sh...  77.8 us
    dot_general x28, matrix products, mix(): return jnp.einsum(form, left, right, preferred_element_type=jnp.float32)  54.8 us
    ppermute x4, waiting for transfers between devices, shifted(): lax.ppermute(value, axis, [(source, source + steps) for source in range(l...  21.3 us
    dot_general x4, matrix products, layer_forward(): joined = jnp.dot(normed, w_qkv, preferred_element_type=jnp.float32)  12.7 us
    dot_general x4, matrix products, layer_backward(): jnp.dot(grad_in, w_out, preferred_element_type=jnp.float32)  12.2 us
    ppermute x4, starting transfers between devices, shifted(): lax.ppermute(value, axis, [(source, source + steps) for source in range(l...  8.46 us
    neg x16, other arithmetic, rotate_half(): return jnp.concatenate([-second, first], axis=-1)  7.62 us
  transfers between devices with their start and end apart: 4, of which 3 were waited for; matrix products, arithmetic and copies ran while one was open for 10% of the time, Pallas kernels for 0%

profile of v2, /device:TPU:0, one launch (start us, length us, event | category | flops | bytes accessed | tf_op | source)
XLA Modules:
  0.0 333.5 jit_solution(17394269831220937738)
XLA Ops:
  0.7 1.5 fusion.60
  3.4 77.8 %shard_map.84 = (bf16[2048,1536]{1,0:T(8,128)(2,1)}, bf16[2048,1024]{1,0:T(8,128)(2,1)}, bf16[256,128]{1,0:T(8,128)(2,1)}) custom-call(bf16[128,1536]{1,0:T(8,128)(2,1)} %bitcast.386, bf16[128,1024]{1,0:T(8,128)(2,1)} %bitcast.426, bf16[16,128]{1,0:T(8,128)(2,1)} %broadcast_in_dim.31.gain), custom_call_target="tpu_custom_call" | custom-call | tf_op jit(solution)/shard_map/pallas_call | solution.py:312
  82.0 4.0 %fusion.142 = f32[128,1536]{1,0:T(8,128)S(1)} fusion(bf16[2048,1536]{1,0:T(8,128)(2,1)} %get-tuple-element.10, f32[2048]{0:T(1024)S(1)} %bitcast.417, f32[128]{0:T(128)S(1)} %add_rsqrt_fusion.3, bf16[2,128,2048]{2,1,0:T(8,128)(2,1)} %param.5), kind=kOutput, calls=%fused_computation.235 | convolution fusion | flops 806354944 | bytes 7610880 | tf_op jit(solution)/shard_map/dot_general | solution.py:57
  87.6 4.5 %fusion.4 = bf16[128,2048]{1,0:T(8,128)(2,1)} fusion(bf16[128,1024]{0,1:T(8,128)(2,1)S(1)} %bitcast.407, bf16[2048,1024]{1,0:T(8,128)(2,1)} %get-tuple-element.11, bf16[2,128,2048]{2,1,0:T(8,128)(2,1)S(1)} %copy-done.2), kind=kOutput, calls=%fused_computation.10 | convolution fusion | flops 537657344 | bytes 5505024 | tf_op jit(solution)/shard_map/sc,dc->sd/dot_general | solution.py:23
  92.1 3.6 %collective-permute-start = (bf16[128,2048]{1,0:T(8,128)(2,1)}, bf16[128,2048]{1,0:T(8,128)(2,1)S(1)}, u32[]{:S(2)}, u32[]{:S(2)}) collective-permute-start(bf16[128,2048]{1,0:T(8,128)(2,1)} %fusion.4), channel_id=1, source_target_pairs={{0,16},{1,17},{2,18},{3,19},{4,20},{5,21},{6,22},{7,23},{8,24},{9,... | collective-permute-start | bytes 1572872 | tf_op jit(solution)/shard_map/ppermute | solution.py:19
  96.3 3.9 %fusion.140 = f32[128,1536]{1,0:T(8,128)S(1)} fusion(bf16[2048,1536]{1,0:T(8,128)(2,1)} %get-tuple-element.10, f32[128]{0:T(128)S(1)} %add_rsqrt_fusion.1, f32[2048]{0:T(1024)S(1)} %bitcast.418, bf16[2,128,2048]{2,1,0:T(8,128)(2,1)S(1)} %copy-done.2), kind=kOutput, calls=%fused_computation.234 | convolution fusion | flops 806354944 | bytes 7610880 | tf_op jit(solution)/shard_map/dot_general | solution.py:57
  102.6 2.1 copy.111
  104.7 4.2 %convolution_convert_fusion.5 = bf16[1024,128]{1,0:T(8,128)(2,1)} fusion(bf16[2048,1024]{1,0:T(8,128)(2,1)} %get-tuple-element.11, bf16[2,128,2048]{2,1,0:T(8,128)(2,1)S(1)} %copy-done.4), kind=kOutput, calls=%fused_computation.87 | convolution fusion | flops 537001984 | bytes 4980736 | tf_op jit(solution)/shard_map/dot_general | solution.py:84
  111.4 4.3 %convolution_convert_fusion.7 = bf16[1024,128]{1,0:T(8,128)(2,1)} fusion(bf16[2048,1024]{1,0:T(8,128)(2,1)} %get-tuple-element.11, bf16[2,128,2048]{2,1,0:T(8,128)(2,1)} %param.6), kind=kOutput, calls=%fused_computation.89 | convolution fusion | flops 537001984 | bytes 4980736 | tf_op jit(solution)/shard_map/dot_general | solution.py:84
  116.5 3.8 %fusion.126 = f32[128,1536]{1,0:T(8,128)S(1)} fusion(bf16[2048,1536]{1,0:T(8,128)(2,1)} %get-tuple-element.10, bf16[128,2048]{1,0:T(8,128)(2,1)S(1)} %collective-permute-done, f32[128]{0:T(128)S(1)} %get-tuple-element.73, f32[2048]{0:T(1024)S(1)} %bitcast.419), kind=kOutput, calls=%fused_computation.209 | convolution fusion | flops 806354944 | bytes 7610880 | tf_op jit(solution)/shard_map/dot_general | solution.py:57
  121.3 1.5 fusion.131
  122.8 2.0 fusion.85
  124.8 1.8 convolution_convert_fusion.1
  127.4 4.5 %fusion.6 = bf16[128,2048]{1,0:T(8,128)(2,1)} fusion(bf16[128,1024]{0,1:T(8,128)(2,1)S(1)} %bitcast.410, bf16[2048,1024]{1,0:T(8,128)(2,1)} %get-tuple-element.11, bf16[2,128,2048]{2,1,0:T(8,128)(2,1)S(1)} %copy-done.2), kind=kOutput, calls=%fused_computation.12 | convolution fusion | flops 537657344 | bytes 5505024 | tf_op jit(solution)/shard_map/sc,dc->sd/dot_general | solution.py:23
  137.0 2.4 broadcast_select_fusion.1
  139.4 1.7 collective-permute-start.1
  142.0 1.8 broadcast_select_fusion.5
  143.8 1.5 slice_negate_fusion.11
  145.4 4.7 %fusion.11 = bf16[1,128,2048]{2,1,0:T(8,128)(2,1)} fusion(bf16[128,2048]{1,0:T(8,128)(2,1)} %fusion.4, bf16[128,1024]{0,1:T(8,128)(2,1)S(1)} %bitcast.398, bf16[2048,1024]{1,0:T(8,128)(2,1)} %get-tuple-element.11, bf16[128,2048]{1,0:T(8,128)(2,1)S(1)} %collective-permute-done, pred[]{:T(512)S(6)} %eq.3), kind=kOutput, calls=%fused_computation.17 | convolution fusion | flops 537919488 | bytes 6029313 | tf_op jit(solution)/shard_map/sc,dc->sd/dot_general | solution.py:23
  150.0 3.0 collective-permute-done.1
  156.2 1.7 fusion.136
  162.9 2.7 fusion.58
  165.7 1.9 convolution_convert_fusion
  167.6 1.5 slice_negate_fusion.9
  170.0 1.5 bitcast_multiply_fusion.4
  172.8 2.3 fusion.81
  175.2 2.3 fusion.73
  177.6 1.6 fusion.72
  179.2 1.5 collective-permute-start.2
  180.7 1.6 collective-permute-start.3
  183.1 1.6 fusion.9
  185.8 2.4 broadcast_select_fusion
  188.2 8.4 %collective-permute-done.2 = bf16[128,2048]{1,0:T(8,128)(2,1)} collective-permute-done((bf16[128,2048]{1,0:T(8,128)(2,1)}, bf16[128,2048]{1,0:T(8,128)(2,1)}, u32[]{:S(2)}, u32[]{:S(2)}) %collective-permute-start.2) | collective-permute-done | bytes 524320 | tf_op jit(solution)/shard_map/ppermute | solution.py:19
  196.6 9.9 %collective-permute-done.3 = bf16[128,2048]{1,0:T(8,128)(2,1)} collective-permute-done((bf16[128,2048]{1,0:T(8,128)(2,1)}, bf16[128,2048]{1,0:T(8,128)(2,1)}, u32[]{:S(2)}, u32[]{:S(2)}) %collective-permute-start.3) | collective-permute-done | bytes 524320 | tf_op jit(solution)/shard_map/ppermute | solution.py:19
  207.8 2.9 convolution_convert_fusion.6
  211.8 2.0 fusion.59
  213.8 2.2 convolution_bitcast_fusion
  215.9 3.0 fusion.55
  219.0 3.1 fusion.42
  224.4 1.6 copy.128
  225.9 2.0 copy.122
  228.0 2.2 convolution_bitcast_fusion.2
  230.1 2.3 fusion.48
  232.5 3.3 broadcast_multiply_fusion.2
  238.8 2.0 bitcast_multiply_fusion.3
  241.9 2.1 copy.110
  246.1 2.0 subtract_convert_fusion.1
  248.1 83.0 %shard_map.85 = (f32[128,1536]{1,0:T(8,128)S(1)}, f32[128,1024]{1,0:T(8,128)S(1)}) custom-call(bf16[256,2048]{1,0:T(8,128)(2,1)S(1)} %pad_maximum_fusion.normed, bf16[256,1536]{1,0:T(8,128)(2,1)S(1)} %maximum_maximum_fusion.joined, bf16[256,2048]{1,0:T(8,128)(2,1)S(1)} %pad_maximum_fusion.1.incoming, bf16[256,1024]{1,0:T(8,128)(2,1)S(1)} %pad_maximum_fusion.6.context), custom_call_target="tpu_custom_call" | custom-call | tf_op jit(solution)/shard_map/pallas_call | solution.py:425
  (219 shorter events, 42.6 us)
Async XLA Ops:
  0.7 86.2 %copy-start.36 = (pred[128,128]{0,1:T(8,128)(4,1)}, pred[128,128]{0,1:T(8,128)(4,1)S(1)}, u32[]{:S(2)}) copy-start(pred[128,128]{0,1:T(8,128)(4,1)S(1)} %iota_compare_fusion) | copy-start | bytes 49156
  2.2 83.8 %copy-start.44 = (f32[128]{0:T(128)}, f32[128]{0:T(128)S(1)}, u32[]{:S(2)}) copy-start(f32[128]{0:T(128)S(1)} %add_rsqrt_fusion.3) | copy-start | bytes 1540
  92.1 23.7 %collective-permute-start = (bf16[128,2048]{1,0:T(8,128)(2,1)}, bf16[128,2048]{1,0:T(8,128)(2,1)S(1)}, u32[]{:S(2)}, u32[]{:S(2)}) collective-permute-start(bf16[128,2048]{1,0:T(8,128)(2,1)} %fusion.4), channel_id=1, source_target_pairs={{0,16},{1,17},{2,18},{3,19},{4,20},{5,21},{6,22},{7,23},{8,24},{9,... | collective-permute-start | bytes 1572872 | tf_op jit(solution)/shard_map/ppermute | solution.py:19
  96.3 8.4 %copy-start.4 = (bf16[2,128,2048]{2,1,0:T(8,128)(2,1)S(1)}, bf16[2,128,2048]{2,1,0:T(8,128)(2,1)}, u32[]{:S(2)}) copy-start(bf16[2,128,2048]{2,1,0:T(8,128)(2,1)} %param.6) | copy-start | bytes 3145732
  102.6 7.2 %copy-start.20 = (f32[128,256]{1,0:T(8,128)S(1)}, f32[128,256]{1,0:T(8,128)}, u32[]{:S(2)}) copy-start(f32[128,256]{1,0:T(8,128)} %slice.218) | copy-start | bytes 393220
  122.8 9.6 %copy-start.29 = (bf16[128,4,64]{0,2,1:T(8,128)(2,1)}, bf16[128,4,64]{0,2,1:T(8,128)(2,1)S(1)}, u32[]{:S(2)}) copy-start(bf16[128,4,64]{0,2,1:T(8,128)(2,1)S(1)} %get-tuple-element.56) | copy-start | bytes 196612
  124.8 9.8 %copy-start.17 = (bf16[128,4,4,64]{0,3,2,1:T(8,128)(2,1)}, bf16[128,4,4,64]{0,3,2,1:T(8,128)(2,1)S(1)}, u32[]{:S(2)}) copy-start(bf16[128,4,4,64]{0,3,2,1:T(8,128)(2,1)S(1)} %get-tuple-element.58) | copy-start | bytes 786436
  124.8 7.1 %copy-start.37 = (pred[128,128]{0,1:T(8,128)(4,1)S(1)}, pred[128,128]{0,1:T(8,128)(4,1)}, u32[]{:S(2)}) copy-start(pred[128,128]{0,1:T(8,128)(4,1)} %copy-done.36) | copy-start | bytes 49156
  132.5 3.3 copy-start.52
  133.9 3.1 copy-start.26
  137.0 16.7 %slice-start = ((s8[6291456]{0:T(1024)(128)(4,1)}), s8[2097152]{0:T(1024)(128)(4,1)S(1)}, s32[]{:S(2)}) async-start(s8[6291456]{0:T(1024)(128)(4,1)} %bitcast.365), calls=%async_computation | async-start | bytes 4194304
  139.4 13.6 %collective-permute-start.1 = (bf16[128,2048]{1,0:T(8,128)(2,1)}, bf16[128,2048]{1,0:T(8,128)(2,1)S(1)}, u32[]{:S(2)}, u32[]{:S(2)}) collective-permute-start(bf16[128,2048]{1,0:T(8,128)(2,1)} %fusion.6), channel_id=1, source_target_pairs={{0,16},{1,17},{2,18},{3,19},{4,20},{5,21},{6,22},{7,23},{8,24},{9,... | collective-permute-start | bytes 1572872 | tf_op jit(solution)/shard_map/ppermute | solution.py:19
  142.0 11.8 %slice-start.1 = ((s8[6291456]{0:T(1024)(128)(4,1)}), s8[4194304]{0:T(1024)(128)(4,1)S(1)}, s32[]{:S(2)}) async-start(s8[6291456]{0:T(1024)(128)(4,1)} %bitcast.365), calls=%async_computation.1 | async-start | bytes 8388608
  155.0 4.1 %copy-start.19 = (bf16[128,256]{0,1:T(8,128)(2,1)}, bf16[128,256]{0,1:T(8,128)(2,1)S(1)}, u32[]{:S(2)}) copy-start(bf16[128,256]{0,1:T(8,128)(2,1)S(1)} %copy.100) | copy-start | bytes 196612
  156.2 5.4 %copy-start.15 = (bf16[128,4,4,64]{0,3,2,1:T(8,128)(2,1)}, bf16[128,4,4,64]{0,3,2,1:T(8,128)(2,1)S(1)}, u32[]{:S(2)}) copy-start(bf16[128,4,4,64]{0,3,2,1:T(8,128)(2,1)S(1)} %fusion.89) | copy-start | bytes 786436
  156.2 5.4 %copy-start.38 = (pred[128,128]{0,1:T(8,128)(4,1)S(1)}, pred[128,128]{0,1:T(8,128)(4,1)}, u32[]{:S(2)}) copy-start(pred[128,128]{0,1:T(8,128)(4,1)} %copy-done.36) | copy-start | bytes 49156
  157.9 3.7 %copy-start.31 = (bf16[128,4,64]{0,2,1:T(8,128)(2,1)}, bf16[128,4,64]{0,2,1:T(8,128)(2,1)S(1)}, u32[]{:S(2)}) copy-start(bf16[128,4,64]{0,2,1:T(8,128)(2,1)S(1)} %get-tuple-element.71) | copy-start | bytes 196612
  159.1 2.5 copy-start.51
  162.9 8.9 %slice-start.2 = ((s8[6291456]{0:T(1024)(128)(4,1)}), s8[2097152]{0:T(1024)(128)(4,1)S(1)}, s32[]{:S(2)}) async-start(s8[6291456]{0:T(1024)(128)(4,1)} %bitcast.367), calls=%async_computation.2 | async-start | bytes 4194304
  169.9 1.8 copy-start.32
  169.9 1.8 copy-start.33
  170.0 1.8 copy-start.40
  170.0 2.9 slice-start.3
  170.0 2.9 copy-start.42
  171.8 3.3 copy-start.21
  171.8 3.3 copy-start.41
  175.1 2.4 copy-start.5
  175.1 2.4 copy-start.49
  175.1 2.4 copy-start.50
  177.5 4.8 %copy-start.3 = (bf16[2,128,2048]{2,1,0:T(8,128)(2,1)S(1)}, bf16[2,128,2048]{2,1,0:T(8,128)(2,1)}, u32[]{:S(2)}) copy-start(bf16[2,128,2048]{2,1,0:T(8,128)(2,1)} %param.5) | copy-start | bytes 3145732
  177.5 4.8 %copy-start.45 = (f32[128]{0:T(128)S(1)}, f32[128]{0:T(128)}, u32[]{:S(2)}) copy-start(f32[128]{0:T(128)} %copy-done.44) | copy-start | bytes 1540
  177.5 4.8 %copy-start.47 = (f32[128]{0:T(128)S(1)}, f32[128]{0:T(128)}, u32[]{:S(2)}) copy-start(f32[128]{0:T(128)} %copy-done.46) | copy-start | bytes 1540
  177.5 5.5 %copy-start.13 = (bf16[128,1024]{1,0:T(8,128)(2,1)S(1)}, bf16[128,1024]{1,0:T(8,128)(2,1)}, u32[]{:S(2)}) copy-start(bf16[128,1024]{1,0:T(8,128)(2,1)} %copy.131) | copy-start | bytes 786436
  177.6 5.5 %copy-start.14 = (bf16[128,1024]{1,0:T(8,128)(2,1)S(1)}, bf16[128,1024]{1,0:T(8,128)(2,1)}, u32[]{:S(2)}) copy-start(bf16[128,1024]{1,0:T(8,128)(2,1)} %copy.132) | copy-start | bytes 786436
  179.2 3.9 %copy-start.16 = (bf16[128,1024]{1,0:T(8,128)(2,1)S(1)}, bf16[128,1024]{1,0:T(8,128)(2,1)}, u32[]{:S(2)}) copy-start(bf16[128,1024]{1,0:T(8,128)(2,1)} %broadcast_select_fusion.5) | copy-start | bytes 786436
  179.2 3.9 %copy-start = (bf16[2048,1024]{1,0:T(8,128)(2,1)S(1)}, bf16[2048,1024]{1,0:T(8,128)(2,1)}, u32[]{:S(2)}) copy-start(bf16[2048,1024]{1,0:T(8,128)(2,1)} %get-tuple-element.11) | copy-start | bytes 12582916
  179.2 4.0 %copy-start.9 = (bf16[128,2048]{1,0:T(8,128)(2,1)S(1)}, bf16[128,2048]{1,0:T(8,128)(2,1)}, u32[]{:S(2)}) copy-start(bf16[128,2048]{1,0:T(8,128)(2,1)} %fusion.6) | copy-start | bytes 1572868
  179.2 17.4 %collective-permute-start.2 = (bf16[128,2048]{1,0:T(8,128)(2,1)}, bf16[128,2048]{1,0:T(8,128)(2,1)}, u32[]{:S(2)}, u32[]{:S(2)}) collective-permute-start(bf16[128,2048]{1,0:T(8,128)(2,1)} %get-tuple-element.20), channel_id=1, source_target_pairs={{16,0},{17,1},{18,2},{19,3},{20,4},{21,5},{22,6},{23,7},{24,8},{25... | collective-permute-start | bytes 1572872 | tf_op jit(solution)/shard_map/ppermute | solution.py:19
  180.7 25.8 %collective-permute-start.3 = (bf16[128,2048]{1,0:T(8,128)(2,1)}, bf16[128,2048]{1,0:T(8,128)(2,1)}, u32[]{:S(2)}, u32[]{:S(2)}) collective-permute-start(bf16[128,2048]{1,0:T(8,128)(2,1)} %get-tuple-element.21), channel_id=1, source_target_pairs={{16,0},{17,1},{18,2},{19,3},{20,4},{21,5},{22,6},{23,7},{24,8},{25... | collective-permute-start | bytes 1572872 | tf_op jit(solution)/shard_map/ppermute | solution.py:19
  183.1 2.7 copy-start.39
  184.8 21.8 %copy-start.6 = (bf16[2,128,2048]{2,1,0:T(8,128)(2,1)S(1)}, bf16[2,128,2048]{2,1,0:T(8,128)(2,1)}, u32[]{:S(2)}) copy-start(bf16[2,128,2048]{2,1,0:T(8,128)(2,1)} %param.6) | copy-start | bytes 3145732
  188.2 22.6 %copy-start.1 = (bf16[2048,1024]{1,0:T(8,128)(2,1)S(1)}, bf16[2048,1024]{1,0:T(8,128)(2,1)}, u32[]{:S(2)}) copy-start(bf16[2048,1024]{1,0:T(8,128)(2,1)} %get-tuple-element.11) | copy-start | bytes 12582916
  215.9 16.5 %copy-start.18 = (bf16[128,4,4,64]{0,3,2,1:T(8,128)(2,1)S(1)}, bf16[128,4,4,64]{0,3,2,1:T(8,128)(2,1)}, u32[]{:S(2)}) copy-start(bf16[128,4,4,64]{0,3,2,1:T(8,128)(2,1)} %copy-done.17) | copy-start | bytes 786436
  232.5 8.4 %copy-start.8 = (f32[4,64,4,128]{3,1,2,0:T(8,128)}, f32[4,64,4,128]{3,1,2,0:T(8,128)S(1)}, u32[]{:S(2)}) copy-start(f32[4,64,4,128]{3,1,2,0:T(8,128)S(1)} %fusion.48) | copy-start | bytes 1572868
  240.9 7.2 %copy-start.22 = (bf16[128,256]{1,0:T(8,128)(2,1)S(1)}, bf16[128,256]{1,0:T(8,128)(2,1)}, u32[]{:S(2)}) copy-start(bf16[128,256]{1,0:T(8,128)(2,1)} %copy.116) | copy-start | bytes 196612
  240.9 7.2 %copy-start.23 = (bf16[128,256]{1,0:T(8,128)(2,1)S(1)}, bf16[128,256]{1,0:T(8,128)(2,1)}, u32[]{:S(2)}) copy-start(bf16[128,256]{1,0:T(8,128)(2,1)} %copy.128) | copy-start | bytes 196612
  246.1 85.1 %copy-start.12 = (bf16[1,128,1536]{2,1,0:T(8,128)(2,1)S(1)}, bf16[1,128,1536]{2,1,0:T(8,128)(2,1)}, u32[]{:S(2)}) copy-start(bf16[1,128,1536]{2,1,0:T(8,128)(2,1)} %param.8) | copy-start | bytes 1179652
  246.1 85.2 %copy-start.48 = (bf16[1,128]{1,0:T(2,128)(2,1)S(1)}, bf16[1,128]{1,0:T(2,128)(2,1)}, u32[]{:S(2)}) copy-start(bf16[1,128]{1,0:T(2,128)(2,1)} %param.7) | copy-start | bytes 772
  (13 other events, 15.7 us)

commit v3 on v2

--- a/solution.py
+++ b/solution.py
@@ -437,6 +437,136 @@
     )(normed, joined, incoming, context)
 
 
+NT = (((1,), (1,)), ((), ()))
+TN = (((0,), (0,)), ((), ()))
+
+
+def dot(left, right, form=(((1,), (0,)), ((), ()))):
+    return lax.dot_general(left, right, form, preferred_element_type=jnp.float32)
+
+
+def turned(values, signed):
+    lane = lax.broadcasted_iota(jnp.int32, values.shape, 1) % HEAD_DIM
+    ahead = pltpu.roll(values, 2 * HEAD_DIM - HEAD_DIM // 2, 1)
+    behind = pltpu.roll(values, HEAD_DIM // 2, 1)
+    return jnp.where(lane < HEAD_DIM // 2, ahead, behind) * signed
+
+
+def heads(ref, group, kv):
+    first = kv * group
+    return jnp.concatenate(
+        [ref[:, h * HEAD_DIM : (h + 1) * HEAD_DIM] for h in range(first, first + group)], axis=0
+    )
+
+
+def norm_scale(values):
+    return lax.rsqrt(jnp.mean(values * values, axis=1, keepdims=True) + 1e-05)
+
+
+def forward_kernel(x, gain, w_qkv, w_out, cosine, signed, out, normed, qkv, probs, context, joined):
+    length = x.shape[0]
+    group, inner, kv_width = HEADS // KV_HEADS, HEADS * HEAD_DIM, KV_HEADS * HEAD_DIM
+    values = x[...].astype(jnp.float32)
+    normed[...] = (values * norm_scale(values) * gain[...]).astype(jnp.bfloat16)
+    joined[...] = dot(normed[...], w_qkv[...])
+    pair = 2 * HEAD_DIM
+    for first in range(0, inner + kv_width, pair):
+        block = joined[:, first : first + pair]
+        qkv[:, first : first + pair] = (
+            block * cosine[...] + turned(block, signed[...])
+        ).astype(jnp.bfloat16)
+    qkv[:, inner + kv_width :] = joined[:, inner + kv_width :].astype(jnp.bfloat16)
+    shape = (group * length, length)
+    row = lax.broadcasted_iota(jnp.int32, shape, 0) % length
+    causal = row >= lax.broadcasted_iota(jnp.int32, shape, 1)
+    for kv in range(KV_HEADS):
+        start = inner + kv * HEAD_DIM
+        key = qkv[:, start : start + HEAD_DIM]
+        value = qkv[:, start + kv_width : start + kv_width + HEAD_DIM]
+        scores = dot(heads(qkv, group, kv), key, NT) * HEAD_DIM ** (-0.5)
+        weights = jnp.where(causal, jnp.exp(scores), 0.0)
+        rounded = (weights * (1.0 / jnp.sum(weights, axis=1, keepdims=True))).astype(jnp.bfloat16)
+        probs[kv] = rounded
+        mixed = dot(rounded, value).astype(jnp.bfloat16)
+        for h in range(group):
+            first = (kv * group + h) * HEAD_DIM
+            context[:, first : first + HEAD_DIM] = mixed[h * length : (h + 1) * length]
+    out[...] = (x[...].astype(jnp.float32) + dot(context[...], w_out[...], NT)).astype(jnp.bfloat16)
+
+
+def backward_kernel(
+    grad_in, x, gain, w_qkv, w_out, cosine, signed, qkv, probs, grad_x, grad_joined, wide, grad_ctx
+):
+    length = x.shape[0]
+    group, inner, kv_width = HEADS // KV_HEADS, HEADS * HEAD_DIM, KV_HEADS * HEAD_DIM
+    grad_ctx[...] = dot(grad_in[...], w_out[...]).astype(jnp.bfloat16)
+    for kv in range(KV_HEADS):
+        start = inner + kv * HEAD_DIM
+        key = qkv[:, start : start + HEAD_DIM]
+        value = qkv[:, start + kv_width : start + kv_width + HEAD_DIM]
+        from_ctx = heads(grad_ctx, group, kv)
+        kept = probs[kv].astype(jnp.float32)
+        grad_probs = dot(from_ctx, value, NT)
+        wide[:, start + kv_width : start + kv_width + HEAD_DIM] = dot(probs[kv], from_ctx, TN)
+        centred = grad_probs - jnp.sum(grad_probs * kept, axis=1, keepdims=True)
+        grad_scores = (kept * centred * HEAD_DIM ** (-0.5)).astype(jnp.bfloat16)
+        grad_query = dot(grad_scores, key)
+        for h in range(group):
+            first = (kv * group + h) * HEAD_DIM
+            wide[:, first : first + HEAD_DIM] = grad_query[h * length : (h + 1) * length]
+        wide[:, start : start + HEAD_DIM] = dot(grad_scores, heads(qkv, group, kv), TN)
+    pair = 2 * HEAD_DIM
+    for first in range(0, inner + kv_width, pair):
+        block = wide[:, first : first + pair]
+        grad_joined[:, first : first + pair] = (
+            block * cosine[...] - turned(block, signed[...])
+        ).astype(jnp.bfloat16)
+    grad_joined[:, inner + kv_width :] = wide[:, inner + kv_width :].astype(jnp.bfloat16)
+    values = x[...].astype(jnp.float32)
+    scale_inv = norm_scale(values)
+    scaled = dot(grad_joined[...], w_qkv[...], NT) * gain[...]
+    centre = scale_inv**3 * jnp.mean(scaled * values, axis=1, keepdims=True)
+    total = scale_inv * scaled - values * centre + grad_in[...].astype(jnp.float32)
+    grad_x[...] = total.astype(jnp.bfloat16)
+
+
+def local_call(kernel, flops, results, scratch, operands):
+    moved = sum(array.size * array.dtype.itemsize for array in operands)
+    return pl.pallas_call(
+        kernel,
+        out_shape=[jax.ShapeDtypeStruct(shape, jnp.bfloat16) for shape in results],
+        in_specs=[pl.BlockSpec(memory_space=pltpu.VMEM)] * len(operands),
+        out_specs=[pl.BlockSpec(memory_space=pltpu.VMEM)] * len(results),
+        scratch_shapes=scratch,
+        cost_estimate=pl.CostEstimate(flops=flops, bytes_accessed=moved, transcendentals=0),
+        compiler_params=pltpu.CompilerParams(vmem_limit_bytes=40 * 1024 * 1024),
+    )(*operands)
+
+
+def run_forward(x, weights):
+    length, width = x.shape
+    columns, inner = weights[1].shape[1], weights[2].shape[1]
+    probs = (KV_HEADS, HEADS // KV_HEADS * length, length)
+    results = [(length, width), (length, width), (length, columns), probs, (length, inner)]
+    scratch = [pltpu.VMEM((length, columns), jnp.float32)]
+    flops = 2 * length * width * (columns + inner)
+    out, normed, qkv, probs, context = local_call(
+        forward_kernel, flops, results, scratch, (x, *weights)
+    )
+    return (out, x, normed, qkv, probs, context)
+
+
+def run_backward(grad_in, x, qkv, probs, weights):
+    length, width = x.shape
+    columns, inner = weights[1].shape[1], weights[2].shape[1]
+    scratch = [pltpu.VMEM((length, columns), jnp.float32), pltpu.VMEM((length, inner), jnp.bfloat16)]
+    flops = 2 * length * width * (columns + inner)
+    results = [(length, width), (length, columns)]
+    return local_call(
+        backward_kernel, flops, results, scratch, (grad_in, x, *weights, qkv, probs)
+    )
+
+
 def pick(first, own, other):
     return jax.tree.map(lambda left, right: jnp.where(first, left, right), own, other)
 
@@ -446,24 +576,26 @@
     full_qkv, full_out, full_gain = gather(w_qkv[0], w_out[0], gains[0])
     micro_count, length, width = inputs.shape
     cosine, sine = rope_tables(length)
-    weights = (full_gain, full_qkv, full_out, cosine, sine)
+    half = HEAD_DIM // 2
+    cosine = jnp.concatenate([cosine, cosine], axis=1)
+    signed = jnp.concatenate([-sine[:, :half], sine[:, half:]] * 2, axis=1)
+    weights = (full_gain.astype(jnp.float32)[None], full_qkv, full_out, cosine, signed)
     early, sent = [], []
     for micro in range(micro_count):
-        out, saved = layer_forward(inputs[micro], *weights)
-        early.append((out, saved))
-        sent.append(shifted(out, "pp", 1))
+        early.append(run_forward(inputs[micro], weights))
+        sent.append(shifted(early[-1][0], "pp", 1))
     late, back = [], []
     for micro in range(micro_count):
-        out, saved = layer_forward(sent[micro], *weights)
-        grad_x = layer_backward(cotangent[micro], saved, *weights)[0]
-        late.append((out, saved))
+        late.append(run_forward(sent[micro], weights))
+        _, x, _, qkv, probs, _ = late[-1]
+        grad_x = run_backward(cotangent[micro], x, qkv, probs, weights)[0]
         back.append(shifted(grad_x, "pp", -1))
     kept = []
     for micro in range(micro_count):
-        out, saved = pick(first, early[micro], late[micro])
+        out, x, normed, qkv, probs, context = pick(first, early[micro], late[micro])
         grad_in = jnp.where(first, back[micro], cotangent[micro])
-        grad_joined = layer_backward(grad_in, saved, *weights)[1]
-        kept.append((out, saved[2], grad_joined, grad_in, saved[7]))
+        grad_joined = run_backward(grad_in, x, qkv, probs, weights)[1]
+        kept.append((out, normed, grad_joined, grad_in, context))
     outputs, normed, joined, incoming, context = zip(*kept)
     return finish(outputs, normed, joined, incoming, context, gains, w_qkv)
 

time: 335 us -> 251 us (0.75)
  matrix products: 86.1 us -> 0 us
  Pallas kernels: 161 us -> 195 us
  other arithmetic: 30.9 us -> 5.3 us
  local copies, waits for them, and re-layouts: 24.1 us -> 18.8 us
    dot_general x36 -> x0, matrix products: 79.7 us -> none  [the longest x28 54.8 us: mix(): return jnp.einsum(form, left, right, preferred_element_type=jnp.float32)]
    pallas_call x0 -> x8, Pallas kernels: none -> 34.6 us  [local_call(): pl.pallas_call(kernel, out_shape=[jax.ShapeDtypeStruct(shape, jnp.bfloat1...]
    unnamed x116 -> x30, local copies, waits for them, and re-layouts: 3.83 us -> 14.9 us
    neg x16 -> x1, other arithmetic: 7.62 us -> 0.26 us  [two_sections(): signed = jnp.concatenate([-sine[:, :half], sine[:, half:]] * 2, axis=1)]
    reshape x6 -> x0, local copies, waits for them, and re-layouts: 6.62 us -> none  [the longest x2 4.1 us: layer_backward(): mix('kgst,tkh->skgh', grad_scores, keys).reshape(length, HEADS, HEAD_DIM)]
    div x4 -> x0, matrix products: 6.43 us -> none  [layer_forward(): weights / jnp.sum(weights, axis=-1, keepdims=True)]
    convert_element_type x7 -> x1, other arithmetic: 6.04 us -> 0.01 us  [two_sections(): full_gain.astype(jnp.float32)[None]]
    convert_element_type x6 -> x0, local copies, waits for them, and re-layouts: 3.74 us -> none  [the longest x4 3.41 us: layer_forward(): mix('kgst,tkh->skgh', probs, values_v).reshape(length, inner)]
  transfers between devices with their start and end apart: 4 -> 4, of which waited for: 3 -> 4; matrix products, arithmetic and copies ran while one was open for 10% -> 2% of each run, Pallas kernels for 0% -> 5%
where the time goes in v3:
time: 251 us; the launch traced here: 250 us
  Pallas kernels  195 us (78%)
  waiting for transfers between devices  21.8 us (9%)
  local copies, waits for them, and re-layouts  18.8 us (7%)
  starting transfers between devices  7.88 us (3%)
  other arithmetic  5.3 us (2%)
    pallas_call x1, Pallas kernels, reduce_terms(): pl.pallas_call(functools.partial(reduce_kernel, count), out_shape=[jax.Sh...  83 us
    pallas_call x1, Pallas kernels, gather(): pl.pallas_call(functools.partial(gather_kernel, count), out_shape=[jax.Sh...  77.8 us
    pallas_call x8, Pallas kernels, local_call(): pl.pallas_call(kernel, out_shape=[jax.ShapeDtypeStruct(shape, jnp.bfloat1...  34.6 us
    ppermute x4, waiting for transfers between devices, shifted(): lax.ppermute(value, axis, [(source, source + steps) for source in range(l...  21.8 us
    unnamed x30, local copies, waits for them, and re-layouts  14.9 us
    ppermute x4, starting transfers between devices, shifted(): lax.ppermute(value, axis, [(source, source + steps) for source in range(l...  7.88 us
  transfers between devices with their start and end apart: 4, of which 4 were waited for; matrix products, arithmetic and copies ran while one was open for 2% of the time, Pallas kernels for 5%

profile of v3, /device:TPU:0, one launch (start us, length us, event | category | flops | bytes accessed | tf_op | source)
XLA Modules:
  0.0 250.1 jit_solution(6789147520240681292)
XLA Ops:
  0.7 1.3 slice_bitcast_fusion.3
  1.9 0.6 broadcast_in_dim.21.gain
  2.5 77.8 %shard_map.84 = (bf16[2048,1536]{1,0:T(8,128)(2,1)}, bf16[2048,1024]{1,0:T(8,128)(2,1)}, bf16[256,128]{1,0:T(8,128)(2,1)}) custom-call(bf16[128,1536]{1,0:T(8,128)(2,1)} %bitcast.42, bf16[128,1024]{1,0:T(8,128)(2,1)} %bitcast.43, bf16[16,128]{1,0:T(8,128)(2,1)} %broadcast_in_dim.21.gain), custom_call_target="tpu_custom_call" | custom-call | tf_op jit(solution)/shard_map/pallas_call | solution.py:312
  80.3 0.8 slice.22
  81.1 0.3 fusion.2
  81.3 0.2 pad_maximum_fusion.4
  81.5 2.8 %copy-done = bf16[2048,1536]{1,0:T(8,128)(2,1)S(1)} copy-done((bf16[2048,1536]{1,0:T(8,128)(2,1)S(1)}, bf16[2048,1536]{1,0:T(8,128)(2,1)}, u32[]{:S(2)}) %copy-start) | copy-done | bytes 6291480
  84.3 2.2 copy-done.2
  86.5 4.1 %shard_map.87 = (bf16[128,2048]{1,0:T(8,128)(2,1)}, bf16[128,2048]{1,0:T(8,128)(2,1)S(1)}, bf16[128,1536]{1,0:T(8,128)(2,1)S(1)}, bf16[4,512,128]{2,1,0:T(8,128)(2,1)S(1)}, bf16[128,1024]{1,0:T(8,128)(2,1)S(1)}) custom-call(bf16[128,2048]{1,0:T(8,128)(2,1)S(1)} %get-tuple-element.69.x, f32[1,2048]{1,0:T(1,128)S(1)} %bitcast.33, ...), custom_call_target="tpu_custom_call" | custom-call | flops 1342177280 | bytes 11149312 | tf_op jit(solution)/shard_map/pallas_call | solution.py:535
  90.6 0.7 copy-done.4
  91.3 3.5 %collective-permute-start.1 = (bf16[128,2048]{1,0:T(8,128)(2,1)}, bf16[128,2048]{1,0:T(8,128)(2,1)S(1)}, u32[]{:S(2)}, u32[]{:S(2)}) collective-permute-start(bf16[128,2048]{1,0:T(8,128)(2,1)} %get-tuple-element.38), channel_id=1, source_target_pairs={{0,16},{1,17},{2,18},{3,19},{4,20},{5,21},{6,22},{7,23},{8,24},{9,... | collective-permute-start | bytes 1572872 | tf_op jit(solution)/shard_map/ppermute | solution.py:19
  94.8 4.1 %shard_map.85 = (bf16[128,2048]{1,0:T(8,128)(2,1)}, bf16[128,2048]{1,0:T(8,128)(2,1)S(1)}, bf16[128,1536]{1,0:T(8,128)(2,1)S(1)}, bf16[4,512,128]{2,1,0:T(8,128)(2,1)S(1)}, bf16[128,1024]{1,0:T(8,128)(2,1)S(1)}) custom-call(bf16[128,2048]{1,0:T(8,128)(2,1)S(1)} %get-tuple-element.68.x, f32[1,2048]{1,0:T(1,128)S(1)} %bitcast.34, ...), custom_call_target="tpu_custom_call" | custom-call | flops 1342177280 | bytes 11149312 | tf_op jit(solution)/shard_map/pallas_call | solution.py:535
  98.9 0.8 copy-done.6
  99.7 0.7 copy-done.8
  100.4 1.5 collective-permute-start
  101.9 1.3 slice_bitcast_fusion.1
  103.2 4.1 %collective-permute-done.1.x = bf16[128,2048]{1,0:T(8,128)(2,1)S(1)} collective-permute-done((bf16[128,2048]{1,0:T(8,128)(2,1)}, bf16[128,2048]{1,0:T(8,128)(2,1)S(1)}, u32[]{:S(2)}, u32[]{:S(2)}) %collective-permute-start.1) | collective-permute-done | bytes 524320 | tf_op jit(solution)/shard_map/ppermute | solution.py:19
  107.3 2.8 %copy-done.1 = bf16[2048,1536]{1,0:T(8,128)(2,1)S(1)} copy-done((bf16[2048,1536]{1,0:T(8,128)(2,1)S(1)}, bf16[2048,1536]{1,0:T(8,128)(2,1)}, u32[]{:S(2)}) %copy-start.1) | copy-done | bytes 6291480
  110.1 2.2 copy-done.3
  112.3 3.3 %shard_map.88 = (bf16[128,2048]{1,0:T(8,128)(2,1)S(1)}, bf16[128,2048]{1,0:T(8,128)(2,1)S(1)}, bf16[128,1536]{1,0:T(8,128)(2,1)S(1)}, bf16[4,512,128]{2,1,0:T(8,128)(2,1)S(1)}, bf16[128,1024]{1,0:T(8,128)(2,1)S(1)}) custom-call(bf16[128,2048]{1,0:T(8,128)(2,1)S(1)} %collective-permute-done.1.x, f32[1,2048]{1,0:T(1,128)S(1)} %bitcast.35, ...), custom_call_target="tpu_custom_call" | custom-call | flops 1342177280 | bytes 11149312 | tf_op jit(solution)/shard_map/pallas_call | solution.py:535
  115.6 1.1 select_bitcast_fusion
  116.7 1.4 collective-permute-done.x
  118.1 3.3 %shard_map.86 = (bf16[128,2048]{1,0:T(8,128)(2,1)S(1)}, bf16[128,2048]{1,0:T(8,128)(2,1)S(1)}, bf16[128,1536]{1,0:T(8,128)(2,1)S(1)}, bf16[4,512,128]{2,1,0:T(8,128)(2,1)S(1)}, bf16[128,1024]{1,0:T(8,128)(2,1)S(1)}) custom-call(bf16[128,2048]{1,0:T(8,128)(2,1)S(1)} %collective-permute-done.x, f32[1,2048]{1,0:T(1,128)S(1)} %bitcast.36, ...), custom_call_target="tpu_custom_call" | custom-call | flops 1342177280 | bytes 11149312 | tf_op jit(solution)/shard_map/pallas_call | solution.py:535
  121.5 1.1 select_bitcast_fusion.1
  122.6 4.5 %shard_map.89 = (bf16[128,2048]{1,0:T(8,128)(2,1)S(1)}, bf16[128,1536]{1,0:T(8,128)(2,1)}) custom-call(bf16[128,2048]{1,0:T(8,128)(2,1)S(1)} %get-tuple-element.66.grad_in, bf16[128,2048]{1,0:T(8,128)(2,1)S(1)} %collective-permute-done.x, f32[1,2048]{1,0:T(1,128)S(1)} %bitcast.37, bf16[2048,1536]{1,0:T(8,128)(2,1)S(1)} %copy-done.1, ...), custom_call_target="tpu_custom_call" | custom-call | flops 1342177280 | bytes 12591104 | tf_op jit(solution)/shard_map/pallas_call | solution.py:535
  127.1 1.3 collective-permute-start.2
  128.4 4.5 %shard_map.91 = (bf16[128,2048]{1,0:T(8,128)(2,1)S(1)}, bf16[128,1536]{1,0:T(8,128)(2,1)}) custom-call(bf16[128,2048]{1,0:T(8,128)(2,1)S(1)} %get-tuple-element.67.grad_in, bf16[128,2048]{1,0:T(8,128)(2,1)S(1)} %collective-permute-done.1.x, f32[1,2048]{1,0:T(1,128)S(1)} %bitcast.38, bf16[2048,1536]{1,0:T(8,128)(2,1)S(1)} %copy-done.1, ...), custom_call_target="tpu_custom_call" | custom-call | flops 1342177280 | bytes 12591104 | tf_op jit(solution)/shard_map/pallas_call | solution.py:535
  133.0 1.6 collective-permute-start.3
  134.7 0.1 broadcast_select_fusion.probs
  134.8 0.1 broadcast_select_fusion.1.probs
  134.9 1.1 maximum_bitcast_fusion
  136.0 0.1 broadcast_select_fusion.6
  136.1 0.1 broadcast_select_fusion.7
  136.1 0.1 pad_maximum_fusion.normed
  136.3 0.7 copy-done.9
  137.1 0.3 copy-done.10
  137.4 0.1 broadcast_select_fusion.4
  137.5 6.3 %collective-permute-done.2 = bf16[128,2048]{1,0:T(8,128)(2,1)S(1)} collective-permute-done((bf16[128,2048]{1,0:T(8,128)(2,1)S(1)}, bf16[128,2048]{1,0:T(8,128)(2,1)S(1)}, u32[]{:S(2)}, u32[]{:S(2)}) %collective-permute-start.2) | collective-permute-done | bytes 524320 | tf_op jit(solution)/shard_map/ppermute | solution.py:19
  143.9 9.9 %collective-permute-done.3 = bf16[128,2048]{1,0:T(8,128)(2,1)S(1)} collective-permute-done((bf16[128,2048]{1,0:T(8,128)(2,1)S(1)}, bf16[128,2048]{1,0:T(8,128)(2,1)S(1)}, u32[]{:S(2)}, u32[]{:S(2)}) %collective-permute-start.3) | collective-permute-done | bytes 524320 | tf_op jit(solution)/shard_map/ppermute | solution.py:19
  153.8 0.1 broadcast_select_fusion.5
  153.9 0.1 pad_maximum_fusion.1.incoming
  154.0 5.3 %shard_map.92 = (bf16[128,2048]{1,0:T(8,128)(2,1)}, bf16[128,1536]{1,0:T(8,128)(2,1)S(1)}) custom-call(bf16[128,2048]{1,0:T(8,128)(2,1)S(1)} %get-tuple-element.65.grad_in, bf16[128,2048]{1,0:T(8,128)(2,1)S(1)} %get-tuple-element.63.x, f32[1,2048]{1,0:T(1,128)S(1)} %bitcast.39, bf16[2048,1536]{1,0:T(8,128)(2,1)S(1)} %copy-done.1, ...), custom_call_target="tpu_custom_call" | custom-call | flops 1342177280 | bytes 12591104 | tf_op jit(solution)/shard_map/pallas_call | solution.py:535
  159.3 5.3 %shard_map.90 = (bf16[128,2048]{1,0:T(8,128)(2,1)}, bf16[128,1536]{1,0:T(8,128)(2,1)S(1)}) custom-call(bf16[128,2048]{1,0:T(8,128)(2,1)S(1)} %get-tuple-element.64.grad_in, bf16[128,2048]{1,0:T(8,128)(2,1)S(1)} %get-tuple-element.62.x, f32[1,2048]{1,0:T(1,128)S(1)} %bitcast.40, bf16[2048,1536]{1,0:T(8,128)(2,1)S(1)} %copy-done.1, ...), custom_call_target="tpu_custom_call" | custom-call | flops 1342177280 | bytes 12591104 | tf_op jit(solution)/shard_map/pallas_call | solution.py:535
  164.7 83.0 %shard_map.93 = (f32[128,1536]{1,0:T(8,128)S(1)}, f32[128,1024]{1,0:T(8,128)S(1)}) custom-call(bf16[256,2048]{1,0:T(8,128)(2,1)S(1)} %pad_maximum_fusion.normed, bf16[256,1536]{1,0:T(8,128)(2,1)S(1)} %pad_maximum_fusion.2.joined, bf16[256,2048]{1,0:T(8,128)(2,1)S(1)} %pad_maximum_fusion.1.incoming, bf16[256,1024]{1,0:T(8,128)(2,1)S(1)} %pad_maximum_fusion.3.context), custom_call_target="tpu_custom_call" | custom-call | tf_op jit(solution)/shard_map/pallas_call | solution.py:425
  247.7 0.2 multiply_reduce_fusion
  247.9 0.5 bitcast_divide_fusion
  248.4 0.9 copy.14
  249.3 0.8 copy.15
  (27 shorter events, 0.3 us)
Async XLA Ops:
  0.6 1.3 copy-start.13
  81.5 2.8 %copy-start = (bf16[2048,1536]{1,0:T(8,128)(2,1)S(1)}, bf16[2048,1536]{1,0:T(8,128)(2,1)}, u32[]{:S(2)}) copy-start(bf16[2048,1536]{1,0:T(8,128)(2,1)} %get-tuple-element.34.w_qkv) | copy-start | bytes 18874372
  84.3 2.2 copy-start.2
  90.6 0.7 copy-start.4
  91.3 16.0 %collective-permute-start.1 = (bf16[128,2048]{1,0:T(8,128)(2,1)}, bf16[128,2048]{1,0:T(8,128)(2,1)S(1)}, u32[]{:S(2)}, u32[]{:S(2)}) collective-permute-start(bf16[128,2048]{1,0:T(8,128)(2,1)} %get-tuple-element.38), channel_id=1, source_target_pairs={{0,16},{1,17},{2,18},{3,19},{4,20},{5,21},{6,22},{7,23},{8,24},{9,... | collective-permute-start | bytes 1572872 | tf_op jit(solution)/shard_map/ppermute | solution.py:19
  98.9 0.8 copy-start.6
  99.7 0.7 copy-start.8
  100.4 17.8 %collective-permute-start = (bf16[128,2048]{1,0:T(8,128)(2,1)}, bf16[128,2048]{1,0:T(8,128)(2,1)S(1)}, u32[]{:S(2)}, u32[]{:S(2)}) collective-permute-start(bf16[128,2048]{1,0:T(8,128)(2,1)} %get-tuple-element.36), channel_id=1, source_target_pairs={{0,16},{1,17},{2,18},{3,19},{4,20},{5,21},{6,22},{7,23},{8,24},{9,... | collective-permute-start | bytes 1572872 | tf_op jit(solution)/shard_map/ppermute | solution.py:19
  107.3 2.8 %copy-start.1 = (bf16[2048,1536]{1,0:T(8,128)(2,1)S(1)}, bf16[2048,1536]{1,0:T(8,128)(2,1)}, u32[]{:S(2)}) copy-start(bf16[2048,1536]{1,0:T(8,128)(2,1)} %get-tuple-element.34.w_qkv) | copy-start | bytes 18874372
  110.1 2.2 copy-start.3
  127.1 16.7 %collective-permute-start.2 = (bf16[128,2048]{1,0:T(8,128)(2,1)S(1)}, bf16[128,2048]{1,0:T(8,128)(2,1)S(1)}, u32[]{:S(2)}, u32[]{:S(2)}) collective-permute-start(bf16[128,2048]{1,0:T(8,128)(2,1)S(1)} %get-tuple-element.46), channel_id=1, source_target_pairs={{16,0},{17,1},{18,2},{19,3},{20,4},{21,5},{22,6},{23,7},{24,8},{25... | collective-permute-start | bytes 1572872 | tf_op jit(solution)/shard_map/ppermute | solution.py:19
  128.4 6.2 %copy-start.5 = (bf16[128,1536]{1,0:T(8,128)(2,1)S(1)}, bf16[128,1536]{1,0:T(8,128)(2,1)}, u32[]{:S(2)}) copy-start(bf16[128,1536]{1,0:T(8,128)(2,1)} %copy-done.4) | copy-start | bytes 1179652
  133.0 1.8 copy-start.7
  133.0 20.8 %collective-permute-start.3 = (bf16[128,2048]{1,0:T(8,128)(2,1)S(1)}, bf16[128,2048]{1,0:T(8,128)(2,1)S(1)}, u32[]{:S(2)}, u32[]{:S(2)}) collective-permute-start(bf16[128,2048]{1,0:T(8,128)(2,1)S(1)} %get-tuple-element.52), channel_id=1, source_target_pairs={{16,0},{17,1},{18,2},{19,3},{20,4},{21,5},{22,6},{23,7},{24,8},{25... | collective-permute-start | bytes 1572872 | tf_op jit(solution)/shard_map/ppermute | solution.py:19
  136.0 1.0 copy-start.9
  136.1 1.2 copy-start.10
  137.0 16.8 %copy-start.11 = (bf16[2,128,2048]{2,1,0:T(8,128)(2,1)S(1)}, bf16[2,128,2048]{2,1,0:T(8,128)(2,1)}, u32[]{:S(2)}) copy-start(bf16[2,128,2048]{2,1,0:T(8,128)(2,1)} %param.6) | copy-start | bytes 3145732
  164.7 83.0 %copy-start.12 = (bf16[1,128,1536]{2,1,0:T(8,128)(2,1)S(1)}, bf16[1,128,1536]{2,1,0:T(8,128)(2,1)}, u32[]{:S(2)}) copy-start(bf16[1,128,1536]{2,1,0:T(8,128)(2,1)} %param.8) | copy-start | bytes 1179652

commit v4 on v3

--- a/solution.py
+++ b/solution.py
@@ -11,6 +11,7 @@
 KV_HEADS = 4
 HEAD_DIM = 64
 MESH = pl.DeviceIdType.MESH
+PIECES = 4
 
 
 def shifted(value, axis, steps):
@@ -251,8 +252,8 @@
     greet(outers, outer, side, core)
     parts = [(gain, full_gain, 0, gain.shape[0])]
     for source, target in ((qkv, full_qkv), (out, full_out)):
-        half = source.shape[0] // 2
-        parts += [(source, target, 0, half), (source, target, half, half)]
+        size = source.shape[0] // 4
+        parts += [(source, target, k * size, size) for k in range(4)]
     beside, partner = at(outer, 1 - side, core), at(outer, side, 1 - core)
 
     def rows(part, owner):
@@ -260,55 +261,85 @@
         first = pl.multiple_of(owner * source.shape[0] + start, 16)
         return target.at[pl.ds(first, size)]
 
-    started, local = [], []
-
-    def send(source, target, send_sem, recv_sem, device):
-        copy = remote(source, target, send_sem, recv_sem, device)
-        copy.start()
-        started.append(copy)
-
+    def origin(way, step):
+        return outer + step if way else outer - step
+
+    def known(way, step):
+        return outer + step < outers if way else outer >= step
+
+    def onward(way, step, j, source, target):
+        ahead = outer - 1 if way else outer + 1
+        device = at((ahead + outers) % outers, side, core)
+        sent, got = z_out.at[way, step, j], z_in.at[way, step + 1, j]
+        return remote(source, target, sent, got, device)
+
+    def across(way, step, j, source, target):
+        return remote(source, target, x_out.at[way, step, j], x_in.at[way, step, j], beside)
+
+    def paired(over, way, step, j, source, target):
+        sent, got = c_out.at[over, way, step, j], c_in.at[over, way, step, j]
+        return remote(source, target, sent, got, partner)
+
+    def can_pass(way):
+        return outer >= 1 if way else outer + 1 < outers
+
+    hops = [(way, step) for step in range(1, outers) for way in range(2)]
     for j, part in enumerate(parts):
         source, target, start, size = part
         block, spot = source.at[pl.ds(start, size)], rows(part, at(outer, side, core))
-        for step in range(1, outers):
-            peer = at((outer + step) % outers, side, core)
-            send(block, spot, z_out.at[step, j], z_in.at[step, j], peer)
-        send(block, spot, x_out.at[0, j], x_in.at[0, j], beside)
-        send(block, spot, c_out.at[0, 0, j], c_in.at[0, 0, j], partner)
-        copy = pltpu.make_async_copy(block, spot, own.at[j])
-        copy.start()
-        local.append(copy)
+        for way in range(2):
+            pl.when(can_pass(way))(onward(way, 0, j, block, spot).start)
+        across(0, 0, j, block, spot).start()
+        paired(0, 0, 0, j, block, spot).start()
+        pltpu.make_async_copy(block, spot, own.at[j]).start()
     for j, part in enumerate(parts):
-        for step in range(1, outers):
-            spot = rows(part, at((outer + outers - step) % outers, side, core))
-            remote(spot, spot, z_out.at[step, j], z_in.at[step, j], beside).wait_recv()
-            send(spot, spot, x_out.at[step, j], x_in.at[step, j], beside)
-            send(spot, spot, c_out.at[0, step, j], c_in.at[0, step, j], partner)
-        for step in range(outers):
-            spot = rows(part, at((outer + outers - step) % outers, 1 - side, core))
-            remote(spot, spot, x_out.at[step, j], x_in.at[step, j], beside).wait_recv()
-            send(spot, spot, c_out.at[1, step, j], c_in.at[1, step, j], partner)
+        for way, step in hops:
+
+            @pl.when(known(way, step))
+            def _(way=way, step=step, j=j, part=part):
+                spot = rows(part, at(origin(way, step), side, core))
+                onward(way, step - 1, j, spot, spot).wait_recv()
+                if step < outers - 1:
+                    pl.when(can_pass(way))(onward(way, step, j, spot, spot).start)
+                across(way, step, j, spot, spot).start()
+                paired(0, way, step, j, spot, spot).start()
+
+        for way, step in [(0, 0)] + hops:
+
+            @pl.when(known(way, step))
+            def _(way=way, step=step, j=j, part=part):
+                spot = rows(part, at(origin(way, step), 1 - side, core))
+                across(way, step, j, spot, spot).wait_recv()
+                paired(1, way, step, j, spot, spot).start()
+
     for j, part in enumerate(parts):
-        for over in range(2):
-            for step in range(outers):
-                origin = at(
-                    (outer + outers - step) % outers, 1 - side if over else side, 1 - core
-                )
-                spot = rows(part, origin)
-                remote(
-                    spot, spot, c_out.at[over, step, j], c_in.at[over, step, j], partner
-                ).wait_recv()
-    for copy in started:
-        copy.wait_send()
-    for copy in local:
-        copy.wait()
+        for way, step in [(0, 0), (1, 0)] + hops:
+
+            @pl.when(known(way, step))
+            def _(way=way, step=step, j=j, part=part):
+                spot = rows(part, at(origin(way, step), side, core))
+                if step < outers - 1:
+                    pl.when(can_pass(way))(onward(way, step, j, spot, spot).wait_send)
+                if (way, step) == (1, 0):
+                    return
+                across(way, step, j, spot, spot).wait_send()
+                for over in range(2):
+                    there = 1 - side if over else side
+                    landed = rows(part, at(origin(way, step), there, 1 - core))
+                    copy = paired(over, way, step, j, landed, landed)
+                    copy.wait_recv()
+                    copy.wait_send()
+
+        source, target, start, size = part
+        block, spot = source.at[pl.ds(start, size)], rows(part, at(outer, side, core))
+        pltpu.make_async_copy(block, spot, own.at[j]).wait()
 
 
 def gather(qkv, out, gain):
     count = lax.axis_size("fsdp")
     outers = count // 4
     gain = jnp.broadcast_to(gain[None], (16, gain.shape[0]))
-    sems = [(outers, 5), (outers, 5), (outers, 5), (outers, 5), (2, outers, 5), (2, outers, 5)]
+    sems = [(2, outers, 9)] * 4 + [(2, 2, outers, 9)] * 2
     full_qkv, full_out, full_gain = pl.pallas_call(
         functools.partial(gather_kernel, count),
         out_shape=[
@@ -317,7 +348,7 @@
         ],
         in_specs=[pl.BlockSpec(memory_space=pl.ANY)] * 3,
         out_specs=[pl.BlockSpec(memory_space=pl.ANY)] * 3,
-        scratch_shapes=[pltpu.SemaphoreType.DMA((5,))]
+        scratch_shapes=[pltpu.SemaphoreType.DMA((9,))]
         + [pltpu.SemaphoreType.DMA(shape) for shape in sems],
         compiler_params=pltpu.CompilerParams(collective_id=0, has_side_effects=True),
     )(qkv, out, gain)
@@ -346,12 +377,19 @@
     def to_core(k):
         return remote(c_buf.at[k], c_got.at[k], c_out.at[k], c_in.at[k], partner)
 
-    def to_side(k):
-        return remote(x_buf.at[k], x_got.at[k], x_out.at[k], x_in.at[k], beside)
-
-    def to_outer(k):
+    part = (width + context.shape[1]) // PIECES
+
+    def cut(p):
+        return slice(p * part, (p + 1) * part)
+
+    def to_side(k, p):
+        source, target = x_buf.at[k, :, cut(p)], x_got.at[k, :, cut(p)]
+        return remote(source, target, x_out.at[k, p], x_in.at[k, p], beside)
+
+    def to_outer(k, p):
         peer = at((outer + k + 1) % outers, side, core)
-        return remote(z_buf.at[k], z_got.at[k], z_out.at[k], z_in.at[k], peer)
+        source, target = z_buf.at[k, :, cut(p)], z_got.at[k, :, cut(p)]
+        return remote(source, target, z_out.at[k, p], z_in.at[k, p], peer)
 
     def wide(ref):
         return ref[...].astype(jnp.float32)
@@ -363,7 +401,8 @@
         @pl.when(k < outers)
         def _():
             x_buf[k % outers] = both
-            to_side(k % outers).start()
+            for p in range(PIECES):
+                to_side(k % outers, p).start()
 
         @pl.when(k >= outers)
         def _():
@@ -387,27 +426,34 @@
     combine(2 * outers - 1)
 
     def two(k, carry):
-        to_side(k).wait_recv()
-        z_buf[k] = (wide(own.at[outers + k]) + wide(x_got.at[k])).astype(jnp.bfloat16)
-        to_outer(k).start()
+        for p in range(PIECES):
+            to_side(k, p).wait_recv()
+            z_buf[k, :, cut(p)] = (
+                own[outers + k, :, cut(p)].astype(jnp.float32)
+                + x_got[k, :, cut(p)].astype(jnp.float32)
+            ).astype(jnp.bfloat16)
+            to_outer(k, p).start()
         return carry
 
     lax.fori_loop(0, outers - 1, two, 0)
     last = outers - 1
-    to_side(last).wait_recv()
+    for p in range(PIECES):
+        to_side(last, p).wait_recv()
+        for k in range(last):
+            to_outer(k, p).wait_recv()
     total = wide(own.at[outers + last]) + wide(x_got.at[last])
     for k in range(last):
-        to_outer(k).wait_recv()
         total += wide(z_got.at[k])
     sum_qkv[...] = total[:, :width]
     sum_out[...] = total[:, width:]
 
     for k in range(2 * outers):
         to_core(k).wait_send()
-    for k in range(outers):
-        to_side(k).wait_send()
-    for k in range(last):
-        to_outer(k).wait_send()
+    for p in range(PIECES):
+        for k in range(outers):
+            to_side(k, p).wait_send()
+        for k in range(last):
+            to_outer(k, p).wait_send()
 
 
 def reduce_terms(normed, joined, incoming, context):
@@ -421,7 +467,7 @@
         return pltpu.VMEM((number, depth, columns), jnp.bfloat16)
 
     numbers = (2 * outers, 2 * outers, 2 * outers, outers, outers, outers - 1, outers - 1)
-    sems = (2 * outers, 2 * outers, outers, outers, outers - 1, outers - 1)
+    sems = [(2 * outers,)] * 2 + [(outers, PIECES)] * 2 + [(outers - 1, PIECES)] * 2
     return pl.pallas_call(
         functools.partial(reduce_kernel, count),
         out_shape=[
@@ -430,7 +476,7 @@
         in_specs=[pl.BlockSpec(memory_space=pltpu.VMEM)] * 4,
         out_specs=[pl.BlockSpec(memory_space=pltpu.VMEM)] * 2,
         scratch_shapes=[slots(number) for number in numbers]
-        + [pltpu.SemaphoreType.DMA((number,)) for number in sems],
+        + [pltpu.SemaphoreType.DMA(shape) for shape in sems],
         compiler_params=pltpu.CompilerParams(
             collective_id=1, has_side_effects=True, vmem_limit_bytes=48 * 1024 * 1024
         ),
@@ -539,7 +585,7 @@
         out_specs=[pl.BlockSpec(memory_space=pltpu.VMEM)] * len(results),
         scratch_shapes=scratch,
         cost_estimate=pl.CostEstimate(flops=flops, bytes_accessed=moved, transcendentals=0),
-        compiler_params=pltpu.CompilerParams(vmem_limit_bytes=40 * 1024 * 1024),
+        compiler_params=pltpu.CompilerParams(vmem_limit_bytes=24 * 1024 * 1024),
     )(*operands)
 
 
@@ -586,10 +632,14 @@
         sent.append(shifted(early[-1][0], "pp", 1))
     late, back = [], []
     for micro in range(micro_count):
-        late.append(run_forward(sent[micro], weights))
+        arrived = sent[micro]
+        if micro > 0:
+            arrived, grad_x = lax.optimization_barrier((arrived, grad_x))
+            back.append(shifted(grad_x, "pp", -1))
+        late.append(run_forward(arrived, weights))
         _, x, _, qkv, probs, _ = late[-1]
         grad_x = run_backward(cotangent[micro], x, qkv, probs, weights)[0]
-        back.append(shifted(grad_x, "pp", -1))
+    back.append(shifted(grad_x, "pp", -1))
     kept = []
     for micro in range(micro_count):
         out, x, normed, qkv, probs, context = pick(first, early[micro], late[micro])

time: 251 us -> 252 us (level); the launches traced: 250 us -> 247 us
  waiting for transfers between devices: 21.8 us -> 17.3 us
  Pallas kernels: 195 us -> 198 us
    pallas_call x1, Pallas kernels: 77.8 us -> 97.7 us  [gather(): pl.pallas_call(functools.partial(gather_kernel, count), out_shape=[jax.Sh...]
    pallas_call x1, Pallas kernels: 83 us -> 66.7 us  [reduce_terms(): pl.pallas_call(functools.partial(reduce_kernel, count), out_shape=[jax.Sh...]
    ppermute x4, waiting for transfers between devices: 21.8 us -> 17.3 us  [shifted(): lax.ppermute(value, axis, [(source, source + steps) for source in range(l...]
    unnamed x30 -> x34, local copies, waits for them, and re-layouts: 14.9 us -> 14.1 us
  transfers between devices with their start and end apart: 4 -> 4, of which waited for: 4 -> 3; matrix products, arithmetic and copies ran while one was open for 2% -> 2% of each run, Pallas kernels for 5% -> 8%
where the time goes in v4:
time: 252 us; the launch traced here: 247 us
  Pallas kernels  198 us (79%)
  local copies, waits for them, and re-layouts  18 us (7%)
  waiting for transfers between devices  17.3 us (7%)
  starting transfers between devices  7.88 us (3%)
  other arithmetic  4.44 us (2%)
    pallas_call x1, Pallas kernels, gather(): pl.pallas_call(functools.partial(gather_kernel, count), out_shape=[jax.Sh...  97.7 us
    pallas_call x1, Pallas kernels, reduce_terms(): pl.pallas_call(functools.partial(reduce_kernel, count), out_shape=[jax.Sh...  66.7 us
    pallas_call x8, Pallas kernels, local_call(): pl.pallas_call(kernel, out_shape=[jax.ShapeDtypeStruct(shape, jnp.bfloat1...  33.9 us
    ppermute x4, waiting for transfers between devices, shifted(): lax.ppermute(value, axis, [(source, source + steps) for source in range(l...  17.3 us
    unnamed x34, local copies, waits for them, and re-layouts  14.1 us
    ppermute x4, starting transfers between devices, shifted(): lax.ppermute(value, axis, [(source, source + steps) for source in range(l...  7.88 us
  transfers between devices with their start and end apart: 4, of which 3 were waited for; matrix products, arithmetic and copies ran while one was open for 2% of the time, Pallas kernels for 8%

profile of v4, /device:TPU:0, one launch (start us, length us, event | category | flops | bytes accessed | tf_op | source)
XLA Modules:
  0.0 247.0 jit_solution(3599564257139314528)
XLA Ops:
  0.7 0.3 fusion.2
  0.9 1.3 slice_bitcast_fusion.3
  2.2 0.6 broadcast_in_dim.21.gain
  2.8 97.7 %shard_map.84 = (bf16[2048,1536]{1,0:T(8,128)(2,1)}, bf16[2048,1024]{1,0:T(8,128)(2,1)}, bf16[256,128]{1,0:T(8,128)(2,1)}) custom-call(bf16[128,1536]{1,0:T(8,128)(2,1)} %bitcast.42, bf16[128,1024]{1,0:T(8,128)(2,1)} %bitcast.43, bf16[16,128]{1,0:T(8,128)(2,1)} %broadcast_in_dim.21.gain), custom_call_target="tpu_custom_call" | custom-call | tf_op jit(solution)/shard_map/pallas_call | solution.py:343
  100.6 0.8 slice.22
  101.3 0.2 pad_maximum_fusion.4
  101.5 2.8 %copy-done = bf16[2048,1536]{1,0:T(8,128)(2,1)S(1)} copy-done((bf16[2048,1536]{1,0:T(8,128)(2,1)S(1)}, bf16[2048,1536]{1,0:T(8,128)(2,1)}, u32[]{:S(2)}) %copy-start) | copy-done | bytes 6291480
  104.3 2.2 copy-done.2
  106.5 4.1 %shard_map.85 = (bf16[128,2048]{1,0:T(8,128)(2,1)}, bf16[128,2048]{1,0:T(8,128)(2,1)S(1)}, bf16[128,1536]{1,0:T(8,128)(2,1)S(1)}, bf16[4,512,128]{2,1,0:T(8,128)(2,1)S(1)}, bf16[128,1024]{1,0:T(8,128)(2,1)S(1)}) custom-call(bf16[128,2048]{1,0:T(8,128)(2,1)S(1)} %get-tuple-element.72.x, f32[1,2048]{1,0:T(1,128)S(1)} %bitcast.33, ...), custom_call_target="tpu_custom_call" | custom-call | flops 1342177280 | bytes 11149312 | tf_op jit(solution)/shard_map/pallas_call | solution.py:581
  110.6 3.5 %collective-permute-start = (bf16[128,2048]{1,0:T(8,128)(2,1)}, bf16[128,2048]{1,0:T(8,128)(2,1)S(1)}, u32[]{:S(2)}, u32[]{:S(2)}) collective-permute-start(bf16[128,2048]{1,0:T(8,128)(2,1)} %get-tuple-element.38), channel_id=1, source_target_pairs={{0,16},{1,17},{2,18},{3,19},{4,20},{5,21},{6,22},{7,23},{8,24},{9,... | collective-permute-start | bytes 1572872 | tf_op jit(solution)/shard_map/ppermute | solution.py:20
  114.1 3.3 %shard_map.87 = (bf16[128,2048]{1,0:T(8,128)(2,1)S(1)}, bf16[128,2048]{1,0:T(8,128)(2,1)S(1)}, bf16[128,1536]{1,0:T(8,128)(2,1)S(1)}, bf16[4,512,128]{2,1,0:T(8,128)(2,1)S(1)}, bf16[128,1024]{1,0:T(8,128)(2,1)S(1)}) custom-call(bf16[128,2048]{1,0:T(8,128)(2,1)S(1)} %get-tuple-element.73.x, f32[1,2048]{1,0:T(1,128)S(1)} %bitcast.34, ...), custom_call_target="tpu_custom_call" | custom-call | flops 1342177280 | bytes 11149312 | tf_op jit(solution)/shard_map/pallas_call | solution.py:581
  117.4 0.0 copy-start.6
  117.4 0.7 copy-done.6
  118.2 0.7 copy-done.10
  118.9 1.5 collective-permute-start.1
  120.4 1.3 slice_bitcast_fusion
  121.7 4.9 %collective-permute-done.x = bf16[128,2048]{1,0:T(8,128)(2,1)S(1)} collective-permute-done((bf16[128,2048]{1,0:T(8,128)(2,1)}, bf16[128,2048]{1,0:T(8,128)(2,1)S(1)}, u32[]{:S(2)}, u32[]{:S(2)}) %collective-permute-start) | collective-permute-done | bytes 524320 | tf_op jit(solution)/shard_map/ppermute | solution.py:20
  126.6 2.8 %copy-done.1 = bf16[2048,1536]{1,0:T(8,128)(2,1)S(1)} copy-done((bf16[2048,1536]{1,0:T(8,128)(2,1)S(1)}, bf16[2048,1536]{1,0:T(8,128)(2,1)}, u32[]{:S(2)}) %copy-start.1) | copy-done | bytes 6291480
  129.4 2.2 copy-done.3
  131.6 3.3 %shard_map.86 = (bf16[128,2048]{1,0:T(8,128)(2,1)S(1)}, bf16[128,2048]{1,0:T(8,128)(2,1)S(1)}, bf16[128,1536]{1,0:T(8,128)(2,1)S(1)}, bf16[4,512,128]{2,1,0:T(8,128)(2,1)S(1)}, bf16[128,1024]{1,0:T(8,128)(2,1)S(1)}) custom-call(bf16[128,2048]{1,0:T(8,128)(2,1)S(1)} %collective-permute-done.x, f32[1,2048]{1,0:T(1,128)S(1)} %bitcast.35, ...), custom_call_target="tpu_custom_call" | custom-call | flops 1342177280 | bytes 11149312 | tf_op jit(solution)/shard_map/pallas_call | solution.py:581
  135.0 0.1 broadcast_select_fusion.1.probs
  135.1 4.5 %shard_map.88 = (bf16[128,2048]{1,0:T(8,128)(2,1)S(1)}, bf16[128,1536]{1,0:T(8,128)(2,1)}) custom-call(bf16[128,2048]{1,0:T(8,128)(2,1)S(1)} %get-tuple-element.71.grad_in, bf16[128,2048]{1,0:T(8,128)(2,1)S(1)} %collective-permute-done.x, f32[1,2048]{1,0:T(1,128)S(1)} %bitcast.36, bf16[2048,1536]{1,0:T(8,128)(2,1)S(1)} %copy-done.1, ...), custom_call_target="tpu_custom_call" | custom-call | flops 1342177280 | bytes 12591104 | tf_op jit(solution)/shard_map/pallas_call | solution.py:581
  139.6 1.1 select_bitcast_fusion.1
  140.8 0.0 copy-start.7
  140.8 1.4 collective-permute-start.2
  142.2 3.3 %shard_map.89 = (bf16[128,2048]{1,0:T(8,128)(2,1)S(1)}, bf16[128,2048]{1,0:T(8,128)(2,1)S(1)}, bf16[128,1536]{1,0:T(8,128)(2,1)S(1)}, bf16[4,512,128]{2,1,0:T(8,128)(2,1)S(1)}, bf16[128,1024]{1,0:T(8,128)(2,1)S(1)}) custom-call(bf16[128,2048]{1,0:T(8,128)(2,1)S(1)} %collective-permute-done.1.x, f32[1,2048]{1,0:T(1,128)S(1)} %bitcast.37, ...), custom_call_target="tpu_custom_call" | custom-call | flops 1342177280 | bytes 11149312 | tf_op jit(solution)/shard_map/pallas_call | solution.py:581
  145.6 4.5 %shard_map.91 = (bf16[128,2048]{1,0:T(8,128)(2,1)S(1)}, bf16[128,1536]{1,0:T(8,128)(2,1)}) custom-call(bf16[128,2048]{1,0:T(8,128)(2,1)S(1)} %get-tuple-element.70.grad_in, bf16[128,2048]{1,0:T(8,128)(2,1)S(1)} %collective-permute-done.1.x, f32[1,2048]{1,0:T(1,128)S(1)} %bitcast.38, bf16[2048,1536]{1,0:T(8,128)(2,1)S(1)} %copy-done.1, ...), custom_call_target="tpu_custom_call" | custom-call | flops 1342177280 | bytes 12591104 | tf_op jit(solution)/shard_map/pallas_call | solution.py:581
  150.2 0.1 broadcast_select_fusion.probs
  150.2 0.1 select_bitcast_fusion
  150.3 1.5 collective-permute-start.3
  151.9 0.1 broadcast_select_fusion.7
  152.0 1.1 maximum_bitcast_fusion
  153.0 0.1 broadcast_select_fusion.6
  153.1 0.1 pad_maximum_fusion.normed
  153.3 1.0 copy-done.12
  154.3 0.2 broadcast_select_fusion.4
  154.5 2.9 %collective-permute-done.2 = bf16[128,2048]{1,0:T(8,128)(2,1)S(1)} collective-permute-done((bf16[128,2048]{1,0:T(8,128)(2,1)S(1)}, bf16[128,2048]{1,0:T(8,128)(2,1)S(1)}, u32[]{:S(2)}, u32[]{:S(2)}) %collective-permute-start.2) | collective-permute-done | bytes 524320 | tf_op jit(solution)/shard_map/ppermute | solution.py:20
  157.3 9.5 %collective-permute-done.3 = bf16[128,2048]{1,0:T(8,128)(2,1)S(1)} collective-permute-done((bf16[128,2048]{1,0:T(8,128)(2,1)S(1)}, bf16[128,2048]{1,0:T(8,128)(2,1)S(1)}, u32[]{:S(2)}, u32[]{:S(2)}) %collective-permute-start.3) | collective-permute-done | bytes 524320 | tf_op jit(solution)/shard_map/ppermute | solution.py:20
  166.8 0.2 broadcast_select_fusion.5
  167.0 0.1 pad_maximum_fusion.1.incoming
  167.1 5.4 %shard_map.92 = (bf16[128,2048]{1,0:T(8,128)(2,1)}, bf16[128,1536]{1,0:T(8,128)(2,1)S(1)}) custom-call(bf16[128,2048]{1,0:T(8,128)(2,1)S(1)} %get-tuple-element.69.grad_in, bf16[128,2048]{1,0:T(8,128)(2,1)S(1)} %get-tuple-element.67.x, f32[1,2048]{1,0:T(1,128)S(1)} %bitcast.39, bf16[2048,1536]{1,0:T(8,128)(2,1)S(1)} %copy-done.1, ...), custom_call_target="tpu_custom_call" | custom-call | flops 1342177280 | bytes 12591104 | tf_op jit(solution)/shard_map/pallas_call | solution.py:581
  172.5 5.3 %shard_map.90 = (bf16[128,2048]{1,0:T(8,128)(2,1)}, bf16[128,1536]{1,0:T(8,128)(2,1)S(1)}) custom-call(bf16[128,2048]{1,0:T(8,128)(2,1)S(1)} %get-tuple-element.68.grad_in, bf16[128,2048]{1,0:T(8,128)(2,1)S(1)} %get-tuple-element.66.x, f32[1,2048]{1,0:T(1,128)S(1)} %bitcast.40, bf16[2048,1536]{1,0:T(8,128)(2,1)S(1)} %copy-done.1, ...), custom_call_target="tpu_custom_call" | custom-call | flops 1342177280 | bytes 12591104 | tf_op jit(solution)/shard_map/pallas_call | solution.py:581
  177.8 0.1 pad_maximum_fusion.2.joined
  177.9 66.7 %shard_map.93 = (f32[128,1536]{1,0:T(8,128)S(1)}, f32[128,1024]{1,0:T(8,128)S(1)}) custom-call(bf16[256,2048]{1,0:T(8,128)(2,1)S(1)} %pad_maximum_fusion.normed, bf16[256,1536]{1,0:T(8,128)(2,1)S(1)} %pad_maximum_fusion.2.joined, bf16[256,2048]{1,0:T(8,128)(2,1)S(1)} %pad_maximum_fusion.1.incoming, bf16[256,1024]{1,0:T(8,128)(2,1)S(1)} %pad_maximum_fusion.3.context), custom_call_target="tpu_custom_call" | custom-call | tf_op jit(solution)/shard_map/pallas_call | solution.py:471
  244.6 0.2 multiply_reduce_fusion
  244.8 0.5 bitcast_divide_fusion
  245.3 0.9 copy.14
  246.2 0.8 copy.15
  (31 shorter events, 0.3 us)
Async XLA Ops:
  0.6 1.6 copy-start.15
  101.5 2.8 %copy-start = (bf16[2048,1536]{1,0:T(8,128)(2,1)S(1)}, bf16[2048,1536]{1,0:T(8,128)(2,1)}, u32[]{:S(2)}) copy-start(bf16[2048,1536]{1,0:T(8,128)(2,1)} %get-tuple-element.36.w_qkv) | copy-start | bytes 18874372
  104.3 2.2 copy-start.2
  110.6 6.8 %copy-start.4 = (bf16[4,512,128]{2,1,0:T(8,128)(2,1)}, bf16[4,512,128]{2,1,0:T(8,128)(2,1)S(1)}, u32[]{:S(2)}) copy-start(bf16[4,512,128]{2,1,0:T(8,128)(2,1)S(1)} %get-tuple-element.52) | copy-start | bytes 1572868
  110.6 6.8 %copy-start.8 = (bf16[128,1536]{1,0:T(8,128)(2,1)}, bf16[128,1536]{1,0:T(8,128)(2,1)S(1)}, u32[]{:S(2)}) copy-start(bf16[128,1536]{1,0:T(8,128)(2,1)S(1)} %get-tuple-element.51) | copy-start | bytes 1179652
  110.6 16.0 %collective-permute-start = (bf16[128,2048]{1,0:T(8,128)(2,1)}, bf16[128,2048]{1,0:T(8,128)(2,1)S(1)}, u32[]{:S(2)}, u32[]{:S(2)}) collective-permute-start(bf16[128,2048]{1,0:T(8,128)(2,1)} %get-tuple-element.38), channel_id=1, source_target_pairs={{0,16},{1,17},{2,18},{3,19},{4,20},{5,21},{6,22},{7,23},{8,24},{9,... | collective-permute-start | bytes 1572872 | tf_op jit(solution)/shard_map/ppermute | solution.py:20
  117.4 0.7 copy-start.6
  118.2 0.7 copy-start.10
  118.9 21.9 %collective-permute-start.1 = (bf16[128,2048]{1,0:T(8,128)(2,1)S(1)}, bf16[128,2048]{1,0:T(8,128)(2,1)S(1)}, u32[]{:S(2)}, u32[]{:S(2)}) collective-permute-start(bf16[128,2048]{1,0:T(8,128)(2,1)S(1)} %get-tuple-element.40), channel_id=1, source_target_pairs={{0,16},{1,17},{2,18},{3,19},{4,20},{5,21},{6,22},{7,23},{8,24},{9,... | collective-permute-start | bytes 1572872 | tf_op jit(solution)/shard_map/ppermute | solution.py:20
  126.6 2.8 %copy-start.1 = (bf16[2048,1536]{1,0:T(8,128)(2,1)S(1)}, bf16[2048,1536]{1,0:T(8,128)(2,1)}, u32[]{:S(2)}) copy-start(bf16[2048,1536]{1,0:T(8,128)(2,1)} %get-tuple-element.36.w_qkv) | copy-start | bytes 18874372
  129.4 2.2 copy-start.3
  131.6 3.3 %copy-start.9 = (bf16[128,1536]{1,0:T(8,128)(2,1)S(1)}, bf16[128,1536]{1,0:T(8,128)(2,1)}, u32[]{:S(2)}) copy-start(bf16[128,1536]{1,0:T(8,128)(2,1)} %copy-done.8) | copy-start | bytes 1179652
  131.6 3.4 %copy-start.5 = (bf16[4,512,128]{2,1,0:T(8,128)(2,1)S(1)}, bf16[4,512,128]{2,1,0:T(8,128)(2,1)}, u32[]{:S(2)}) copy-start(bf16[4,512,128]{2,1,0:T(8,128)(2,1)} %copy-done.4) | copy-start | bytes 1572868
  140.8 4.8 %copy-start.7 = (bf16[128,1536]{1,0:T(8,128)(2,1)S(1)}, bf16[128,1536]{1,0:T(8,128)(2,1)}, u32[]{:S(2)}) copy-start(bf16[128,1536]{1,0:T(8,128)(2,1)} %copy-done.6) | copy-start | bytes 1179652
  140.8 16.6 %collective-permute-start.2 = (bf16[128,2048]{1,0:T(8,128)(2,1)S(1)}, bf16[128,2048]{1,0:T(8,128)(2,1)S(1)}, u32[]{:S(2)}, u32[]{:S(2)}) collective-permute-start(bf16[128,2048]{1,0:T(8,128)(2,1)S(1)} %get-tuple-element.50), channel_id=1, source_target_pairs={{16,0},{17,1},{18,2},{19,3},{20,4},{21,5},{22,6},{23,7},{24,8},{25... | collective-permute-start | bytes 1572872 | tf_op jit(solution)/shard_map/ppermute | solution.py:20
  150.2 1.7 copy-start.11
  150.3 16.5 %collective-permute-start.3 = (bf16[128,2048]{1,0:T(8,128)(2,1)S(1)}, bf16[128,2048]{1,0:T(8,128)(2,1)S(1)}, u32[]{:S(2)}, u32[]{:S(2)}) collective-permute-start(bf16[128,2048]{1,0:T(8,128)(2,1)S(1)} %get-tuple-element.56), channel_id=1, source_target_pairs={{16,0},{17,1},{18,2},{19,3},{20,4},{21,5},{22,6},{23,7},{24,8},{25... | collective-permute-start | bytes 1572872 | tf_op jit(solution)/shard_map/ppermute | solution.py:20
  153.0 1.2 copy-start.12
  153.2 13.6 %copy-start.13 = (bf16[2,128,2048]{2,1,0:T(8,128)(2,1)S(1)}, bf16[2,128,2048]{2,1,0:T(8,128)(2,1)}, u32[]{:S(2)}) copy-start(bf16[2,128,2048]{2,1,0:T(8,128)(2,1)} %param.6) | copy-start | bytes 3145732
  177.9 66.7 %copy-start.14 = (bf16[1,128,1536]{2,1,0:T(8,128)(2,1)S(1)}, bf16[1,128,1536]{2,1,0:T(8,128)(2,1)}, u32[]{:S(2)}) copy-start(bf16[1,128,1536]{2,1,0:T(8,128)(2,1)} %param.8) | copy-start | bytes 1179652

commit v5 on v3

--- a/solution.py
+++ b/solution.py
@@ -11,6 +11,7 @@
 KV_HEADS = 4
 HEAD_DIM = 64
 MESH = pl.DeviceIdType.MESH
+PIECES = 4
 
 
 def shifted(value, axis, steps):
@@ -251,8 +252,8 @@
     greet(outers, outer, side, core)
     parts = [(gain, full_gain, 0, gain.shape[0])]
     for source, target in ((qkv, full_qkv), (out, full_out)):
-        half = source.shape[0] // 2
-        parts += [(source, target, 0, half), (source, target, half, half)]
+        size = source.shape[0] // 2
+        parts += [(source, target, k * size, size) for k in range(2)]
     beside, partner = at(outer, 1 - side, core), at(outer, side, 1 - core)
 
     def rows(part, owner):
@@ -346,12 +347,19 @@
     def to_core(k):
         return remote(c_buf.at[k], c_got.at[k], c_out.at[k], c_in.at[k], partner)
 
-    def to_side(k):
-        return remote(x_buf.at[k], x_got.at[k], x_out.at[k], x_in.at[k], beside)
-
-    def to_outer(k):
+    part = (width + context.shape[1]) // PIECES
+
+    def cut(p):
+        return slice(p * part, (p + 1) * part)
+
+    def to_side(k, p):
+        source, target = x_buf.at[k, :, cut(p)], x_got.at[k, :, cut(p)]
+        return remote(source, target, x_out.at[k, p], x_in.at[k, p], beside)
+
+    def to_outer(k, p):
         peer = at((outer + k + 1) % outers, side, core)
-        return remote(z_buf.at[k], z_got.at[k], z_out.at[k], z_in.at[k], peer)
+        source, target = z_buf.at[k, :, cut(p)], z_got.at[k, :, cut(p)]
+        return remote(source, target, z_out.at[k, p], z_in.at[k, p], peer)
 
     def wide(ref):
         return ref[...].astype(jnp.float32)
@@ -363,7 +371,8 @@
         @pl.when(k < outers)
         def _():
             x_buf[k % outers] = both
-            to_side(k % outers).start()
+            for p in range(PIECES):
+                to_side(k % outers, p).start()
 
         @pl.when(k >= outers)
         def _():
@@ -387,27 +396,34 @@
     combine(2 * outers - 1)
 
     def two(k, carry):
-        to_side(k).wait_recv()
-        z_buf[k] = (wide(own.at[outers + k]) + wide(x_got.at[k])).astype(jnp.bfloat16)
-        to_outer(k).start()
+        for p in range(PIECES):
+            to_side(k, p).wait_recv()
+            z_buf[k, :, cut(p)] = (
+                own[outers + k, :, cut(p)].astype(jnp.float32)
+                + x_got[k, :, cut(p)].astype(jnp.float32)
+            ).astype(jnp.bfloat16)
+            to_outer(k, p).start()
         return carry
 
     lax.fori_loop(0, outers - 1, two, 0)
     last = outers - 1
-    to_side(last).wait_recv()
+    for p in range(PIECES):
+        to_side(last, p).wait_recv()
+        for k in range(last):
+            to_outer(k, p).wait_recv()
     total = wide(own.at[outers + last]) + wide(x_got.at[last])
     for k in range(last):
-        to_outer(k).wait_recv()
         total += wide(z_got.at[k])
     sum_qkv[...] = total[:, :width]
     sum_out[...] = total[:, width:]
 
     for k in range(2 * outers):
         to_core(k).wait_send()
-    for k in range(outers):
-        to_side(k).wait_send()
-    for k in range(last):
-        to_outer(k).wait_send()
+    for p in range(PIECES):
+        for k in range(outers):
+            to_side(k, p).wait_send()
+        for k in range(last):
+            to_outer(k, p).wait_send()
 
 
 def reduce_terms(normed, joined, incoming, context):
@@ -421,7 +437,7 @@
         return pltpu.VMEM((number, depth, columns), jnp.bfloat16)
 
     numbers = (2 * outers, 2 * outers, 2 * outers, outers, outers, outers - 1, outers - 1)
-    sems = (2 * outers, 2 * outers, outers, outers, outers - 1, outers - 1)
+    sems = [(2 * outers,)] * 2 + [(outers, PIECES)] * 2 + [(outers - 1, PIECES)] * 2
     return pl.pallas_call(
         functools.partial(reduce_kernel, count),
         out_shape=[
@@ -430,7 +446,7 @@
         in_specs=[pl.BlockSpec(memory_space=pltpu.VMEM)] * 4,
         out_specs=[pl.BlockSpec(memory_space=pltpu.VMEM)] * 2,
         scratch_shapes=[slots(number) for number in numbers]
-        + [pltpu.SemaphoreType.DMA((number,)) for number in sems],
+        + [pltpu.SemaphoreType.DMA(shape) for shape in sems],
         compiler_params=pltpu.CompilerParams(
             collective_id=1, has_side_effects=True, vmem_limit_bytes=48 * 1024 * 1024
         ),
@@ -539,7 +555,7 @@
         out_specs=[pl.BlockSpec(memory_space=pltpu.VMEM)] * len(results),
         scratch_shapes=scratch,
         cost_estimate=pl.CostEstimate(flops=flops, bytes_accessed=moved, transcendentals=0),
-        compiler_params=pltpu.CompilerParams(vmem_limit_bytes=40 * 1024 * 1024),
+        compiler_params=pltpu.CompilerParams(vmem_limit_bytes=24 * 1024 * 1024),
     )(*operands)
 
 
@@ -586,10 +602,14 @@
         sent.append(shifted(early[-1][0], "pp", 1))
     late, back = [], []
     for micro in range(micro_count):
-        late.append(run_forward(sent[micro], weights))
+        arrived = sent[micro]
+        if micro > 0:
+            arrived, grad_x = lax.optimization_barrier((arrived, grad_x))
+            back.append(shifted(grad_x, "pp", -1))
+        late.append(run_forward(arrived, weights))
         _, x, _, qkv, probs, _ = late[-1]
         grad_x = run_backward(cotangent[micro], x, qkv, probs, weights)[0]
-        back.append(shifted(grad_x, "pp", -1))
+    back.append(shifted(grad_x, "pp", -1))
     kept = []
     for micro in range(micro_count):
         out, x, normed, qkv, probs, context = pick(first, early[micro], late[micro])

time: 251 us -> 237 us (0.944)
  Pallas kernels: 195 us -> 186 us
  waiting for transfers between devices: 21.8 us -> 17.3 us
    pallas_call x1, Pallas kernels: 83 us -> 74.1 us  [reduce_terms(): pl.pallas_call(functools.partial(reduce_kernel, count), out_shape=[jax.Sh...]
    ppermute x4, waiting for transfers between devices: 21.8 us -> 17.3 us  [shifted(): lax.ppermute(value, axis, [(source, source + steps) for source in range(l...]
    unnamed x30 -> x34, local copies, waits for them, and re-layouts: 14.9 us -> 14.1 us
  transfers between devices with their start and end apart: 4 -> 4, of which waited for: 4 -> 3; matrix products, arithmetic and copies ran while one was open for 2% -> 2% of each run, Pallas kernels for 5% -> 8%
where the time goes in v5:
time: 237 us; the launch traced here: 235 us
  Pallas kernels  186 us (78%)
  local copies, waits for them, and re-layouts  18 us (8%)
  waiting for transfers between devices  17.3 us (7%)
  starting transfers between devices  8.14 us (3%)
  other arithmetic  4.44 us (2%)
    pallas_call x1, Pallas kernels, gather(): pl.pallas_call(functools.partial(gather_kernel, count), out_shape=[jax.Sh...  77.8 us
    pallas_call x1, Pallas kernels, reduce_terms(): pl.pallas_call(functools.partial(reduce_kernel, count), out_shape=[jax.Sh...  74.1 us
    pallas_call x8, Pallas kernels, local_call(): pl.pallas_call(kernel, out_shape=[jax.ShapeDtypeStruct(shape, jnp.bfloat1...  33.9 us
    ppermute x4, waiting for transfers between devices, shifted(): lax.ppermute(value, axis, [(source, source + steps) for source in range(l...  17.3 us
    unnamed x34, local copies, waits for them, and re-layouts  14.1 us
    ppermute x4, starting transfers between devices, shifted(): lax.ppermute(value, axis, [(source, source + steps) for source in range(l...  8.14 us
  transfers between devices with their start and end apart: 4, of which 3 were waited for; matrix products, arithmetic and copies ran while one was open for 2% of the time, Pallas kernels for 8%

profile of v5, /device:TPU:0, one launch (start us, length us, event | category | flops | bytes accessed | tf_op | source)
XLA Modules:
  0.0 234.7 jit_solution(10530772600575410757)
XLA Ops:
  0.7 0.3 fusion.2
  0.9 1.3 slice_bitcast_fusion.3
  2.2 0.6 broadcast_in_dim.21.gain
  2.8 77.8 %shard_map.84 = (bf16[2048,1536]{1,0:T(8,128)(2,1)}, bf16[2048,1024]{1,0:T(8,128)(2,1)}, bf16[256,128]{1,0:T(8,128)(2,1)}) custom-call(bf16[128,1536]{1,0:T(8,128)(2,1)} %bitcast.42, bf16[128,1024]{1,0:T(8,128)(2,1)} %bitcast.43, bf16[16,128]{1,0:T(8,128)(2,1)} %broadcast_in_dim.21.gain), custom_call_target="tpu_custom_call" | custom-call | tf_op jit(solution)/shard_map/pallas_call | solution.py:313
  80.6 0.8 slice.22
  81.4 0.2 pad_maximum_fusion.4
  81.5 2.8 %copy-done = bf16[2048,1536]{1,0:T(8,128)(2,1)S(1)} copy-done((bf16[2048,1536]{1,0:T(8,128)(2,1)S(1)}, bf16[2048,1536]{1,0:T(8,128)(2,1)}, u32[]{:S(2)}) %copy-start) | copy-done | bytes 6291480
  84.3 2.2 copy-done.2
  86.5 4.1 %shard_map.85 = (bf16[128,2048]{1,0:T(8,128)(2,1)}, bf16[128,2048]{1,0:T(8,128)(2,1)S(1)}, bf16[128,1536]{1,0:T(8,128)(2,1)S(1)}, bf16[4,512,128]{2,1,0:T(8,128)(2,1)S(1)}, bf16[128,1024]{1,0:T(8,128)(2,1)S(1)}) custom-call(bf16[128,2048]{1,0:T(8,128)(2,1)S(1)} %get-tuple-element.72.x, f32[1,2048]{1,0:T(1,128)S(1)} %bitcast.33, ...), custom_call_target="tpu_custom_call" | custom-call | flops 1342177280 | bytes 11149312 | tf_op jit(solution)/shard_map/pallas_call | solution.py:551
  90.6 3.5 %collective-permute-start = (bf16[128,2048]{1,0:T(8,128)(2,1)}, bf16[128,2048]{1,0:T(8,128)(2,1)S(1)}, u32[]{:S(2)}, u32[]{:S(2)}) collective-permute-start(bf16[128,2048]{1,0:T(8,128)(2,1)} %get-tuple-element.38), channel_id=1, source_target_pairs={{0,16},{1,17},{2,18},{3,19},{4,20},{5,21},{6,22},{7,23},{8,24},{9,... | collective-permute-start | bytes 1572872 | tf_op jit(solution)/shard_map/ppermute | solution.py:20
  94.1 3.3 %shard_map.87 = (bf16[128,2048]{1,0:T(8,128)(2,1)S(1)}, bf16[128,2048]{1,0:T(8,128)(2,1)S(1)}, bf16[128,1536]{1,0:T(8,128)(2,1)S(1)}, bf16[4,512,128]{2,1,0:T(8,128)(2,1)S(1)}, bf16[128,1024]{1,0:T(8,128)(2,1)S(1)}) custom-call(bf16[128,2048]{1,0:T(8,128)(2,1)S(1)} %get-tuple-element.73.x, f32[1,2048]{1,0:T(1,128)S(1)} %bitcast.34, ...), custom_call_target="tpu_custom_call" | custom-call | flops 1342177280 | bytes 11149312 | tf_op jit(solution)/shard_map/pallas_call | solution.py:551
  97.5 0.0 copy-start.6
  97.5 0.7 copy-done.6
  98.2 0.7 copy-done.10
  98.9 1.5 collective-permute-start.1
  100.4 1.3 slice_bitcast_fusion
  101.7 4.9 %collective-permute-done.x = bf16[128,2048]{1,0:T(8,128)(2,1)S(1)} collective-permute-done((bf16[128,2048]{1,0:T(8,128)(2,1)}, bf16[128,2048]{1,0:T(8,128)(2,1)S(1)}, u32[]{:S(2)}, u32[]{:S(2)}) %collective-permute-start) | collective-permute-done | bytes 524320 | tf_op jit(solution)/shard_map/ppermute | solution.py:20
  106.6 2.8 %copy-done.1 = bf16[2048,1536]{1,0:T(8,128)(2,1)S(1)} copy-done((bf16[2048,1536]{1,0:T(8,128)(2,1)S(1)}, bf16[2048,1536]{1,0:T(8,128)(2,1)}, u32[]{:S(2)}) %copy-start.1) | copy-done | bytes 6291480
  109.4 2.2 copy-done.3
  111.6 3.3 %shard_map.86 = (bf16[128,2048]{1,0:T(8,128)(2,1)S(1)}, bf16[128,2048]{1,0:T(8,128)(2,1)S(1)}, bf16[128,1536]{1,0:T(8,128)(2,1)S(1)}, bf16[4,512,128]{2,1,0:T(8,128)(2,1)S(1)}, bf16[128,1024]{1,0:T(8,128)(2,1)S(1)}) custom-call(bf16[128,2048]{1,0:T(8,128)(2,1)S(1)} %collective-permute-done.x, f32[1,2048]{1,0:T(1,128)S(1)} %bitcast.35, ...), custom_call_target="tpu_custom_call" | custom-call | flops 1342177280 | bytes 11149312 | tf_op jit(solution)/shard_map/pallas_call | solution.py:551
  115.0 0.1 broadcast_select_fusion.1.probs
  115.1 4.5 %shard_map.88 = (bf16[128,2048]{1,0:T(8,128)(2,1)S(1)}, bf16[128,1536]{1,0:T(8,128)(2,1)}) custom-call(bf16[128,2048]{1,0:T(8,128)(2,1)S(1)} %get-tuple-element.71.grad_in, bf16[128,2048]{1,0:T(8,128)(2,1)S(1)} %collective-permute-done.x, f32[1,2048]{1,0:T(1,128)S(1)} %bitcast.36, bf16[2048,1536]{1,0:T(8,128)(2,1)S(1)} %copy-done.1, ...), custom_call_target="tpu_custom_call" | custom-call | flops 1342177280 | bytes 12591104 | tf_op jit(solution)/shard_map/pallas_call | solution.py:551
  119.6 1.1 select_bitcast_fusion.1
  120.8 1.6 collective-permute-start.2
  122.4 3.3 %shard_map.89 = (bf16[128,2048]{1,0:T(8,128)(2,1)S(1)}, bf16[128,2048]{1,0:T(8,128)(2,1)S(1)}, bf16[128,1536]{1,0:T(8,128)(2,1)S(1)}, bf16[4,512,128]{2,1,0:T(8,128)(2,1)S(1)}, bf16[128,1024]{1,0:T(8,128)(2,1)S(1)}) custom-call(bf16[128,2048]{1,0:T(8,128)(2,1)S(1)} %collective-permute-done.1.x, f32[1,2048]{1,0:T(1,128)S(1)} %bitcast.37, ...), custom_call_target="tpu_custom_call" | custom-call | flops 1342177280 | bytes 11149312 | tf_op jit(solution)/shard_map/pallas_call | solution.py:551
  125.8 4.5 %shard_map.91 = (bf16[128,2048]{1,0:T(8,128)(2,1)S(1)}, bf16[128,1536]{1,0:T(8,128)(2,1)}) custom-call(bf16[128,2048]{1,0:T(8,128)(2,1)S(1)} %get-tuple-element.70.grad_in, bf16[128,2048]{1,0:T(8,128)(2,1)S(1)} %collective-permute-done.1.x, f32[1,2048]{1,0:T(1,128)S(1)} %bitcast.38, bf16[2048,1536]{1,0:T(8,128)(2,1)S(1)} %copy-done.1, ...), custom_call_target="tpu_custom_call" | custom-call | flops 1342177280 | bytes 12591104 | tf_op jit(solution)/shard_map/pallas_call | solution.py:551
  130.4 0.1 broadcast_select_fusion.probs
  130.5 0.1 select_bitcast_fusion
  130.5 1.6 collective-permute-start.3
  132.1 0.1 broadcast_select_fusion.7
  132.2 1.1 maximum_bitcast_fusion
  133.3 0.1 broadcast_select_fusion.6
  133.4 0.1 pad_maximum_fusion.normed
  133.5 1.0 copy-done.12
  134.5 0.2 broadcast_select_fusion.4
  134.7 2.7 %collective-permute-done.2 = bf16[128,2048]{1,0:T(8,128)(2,1)S(1)} collective-permute-done((bf16[128,2048]{1,0:T(8,128)(2,1)S(1)}, bf16[128,2048]{1,0:T(8,128)(2,1)S(1)}, u32[]{:S(2)}, u32[]{:S(2)}) %collective-permute-start.2) | collective-permute-done | bytes 524320 | tf_op jit(solution)/shard_map/ppermute | solution.py:20
  137.4 9.7 %collective-permute-done.3 = bf16[128,2048]{1,0:T(8,128)(2,1)S(1)} collective-permute-done((bf16[128,2048]{1,0:T(8,128)(2,1)S(1)}, bf16[128,2048]{1,0:T(8,128)(2,1)S(1)}, u32[]{:S(2)}, u32[]{:S(2)}) %collective-permute-start.3) | collective-permute-done | bytes 524320 | tf_op jit(solution)/shard_map/ppermute | solution.py:20
  147.1 0.2 broadcast_select_fusion.5
  147.3 0.1 pad_maximum_fusion.1.incoming
  147.4 5.4 %shard_map.92 = (bf16[128,2048]{1,0:T(8,128)(2,1)}, bf16[128,1536]{1,0:T(8,128)(2,1)S(1)}) custom-call(bf16[128,2048]{1,0:T(8,128)(2,1)S(1)} %get-tuple-element.69.grad_in, bf16[128,2048]{1,0:T(8,128)(2,1)S(1)} %get-tuple-element.67.x, f32[1,2048]{1,0:T(1,128)S(1)} %bitcast.39, bf16[2048,1536]{1,0:T(8,128)(2,1)S(1)} %copy-done.1, ...), custom_call_target="tpu_custom_call" | custom-call | flops 1342177280 | bytes 12591104 | tf_op jit(solution)/shard_map/pallas_call | solution.py:551
  152.8 5.3 %shard_map.90 = (bf16[128,2048]{1,0:T(8,128)(2,1)}, bf16[128,1536]{1,0:T(8,128)(2,1)S(1)}) custom-call(bf16[128,2048]{1,0:T(8,128)(2,1)S(1)} %get-tuple-element.68.grad_in, bf16[128,2048]{1,0:T(8,128)(2,1)S(1)} %get-tuple-element.66.x, f32[1,2048]{1,0:T(1,128)S(1)} %bitcast.40, bf16[2048,1536]{1,0:T(8,128)(2,1)S(1)} %copy-done.1, ...), custom_call_target="tpu_custom_call" | custom-call | flops 1342177280 | bytes 12591104 | tf_op jit(solution)/shard_map/pallas_call | solution.py:551
  158.1 0.1 pad_maximum_fusion.2.joined
  158.2 0.0 copy-start.14
  158.2 74.1 %shard_map.93 = (f32[128,1536]{1,0:T(8,128)S(1)}, f32[128,1024]{1,0:T(8,128)S(1)}) custom-call(bf16[256,2048]{1,0:T(8,128)(2,1)S(1)} %pad_maximum_fusion.normed, bf16[256,1536]{1,0:T(8,128)(2,1)S(1)} %pad_maximum_fusion.2.joined, bf16[256,2048]{1,0:T(8,128)(2,1)S(1)} %pad_maximum_fusion.1.incoming, bf16[256,1024]{1,0:T(8,128)(2,1)S(1)} %pad_maximum_fusion.3.context), custom_call_target="tpu_custom_call" | custom-call | tf_op jit(solution)/shard_map/pallas_call | solution.py:441
  232.4 0.2 multiply_reduce_fusion
  232.5 0.5 bitcast_divide_fusion
  233.0 0.9 copy.14
  233.9 0.8 copy.15
  (31 shorter events, 0.3 us)
Async XLA Ops:
  0.6 1.6 copy-start.15
  81.5 2.8 %copy-start = (bf16[2048,1536]{1,0:T(8,128)(2,1)S(1)}, bf16[2048,1536]{1,0:T(8,128)(2,1)}, u32[]{:S(2)}) copy-start(bf16[2048,1536]{1,0:T(8,128)(2,1)} %get-tuple-element.36.w_qkv) | copy-start | bytes 18874372
  84.3 2.2 copy-start.2
  90.6 6.8 %copy-start.4 = (bf16[4,512,128]{2,1,0:T(8,128)(2,1)}, bf16[4,512,128]{2,1,0:T(8,128)(2,1)S(1)}, u32[]{:S(2)}) copy-start(bf16[4,512,128]{2,1,0:T(8,128)(2,1)S(1)} %get-tuple-element.52) | copy-start | bytes 1572868
  90.6 6.8 %copy-start.8 = (bf16[128,1536]{1,0:T(8,128)(2,1)}, bf16[128,1536]{1,0:T(8,128)(2,1)S(1)}, u32[]{:S(2)}) copy-start(bf16[128,1536]{1,0:T(8,128)(2,1)S(1)} %get-tuple-element.51) | copy-start | bytes 1179652
  90.6 16.0 %collective-permute-start = (bf16[128,2048]{1,0:T(8,128)(2,1)}, bf16[128,2048]{1,0:T(8,128)(2,1)S(1)}, u32[]{:S(2)}, u32[]{:S(2)}) collective-permute-start(bf16[128,2048]{1,0:T(8,128)(2,1)} %get-tuple-element.38), channel_id=1, source_target_pairs={{0,16},{1,17},{2,18},{3,19},{4,20},{5,21},{6,22},{7,23},{8,24},{9,... | collective-permute-start | bytes 1572872 | tf_op jit(solution)/shard_map/ppermute | solution.py:20
  97.5 0.7 copy-start.6
  98.2 0.7 copy-start.10
  98.9 21.9 %collective-permute-start.1 = (bf16[128,2048]{1,0:T(8,128)(2,1)S(1)}, bf16[128,2048]{1,0:T(8,128)(2,1)S(1)}, u32[]{:S(2)}, u32[]{:S(2)}) collective-permute-start(bf16[128,2048]{1,0:T(8,128)(2,1)S(1)} %get-tuple-element.40), channel_id=1, source_target_pairs={{0,16},{1,17},{2,18},{3,19},{4,20},{5,21},{6,22},{7,23},{8,24},{9,... | collective-permute-start | bytes 1572872 | tf_op jit(solution)/shard_map/ppermute | solution.py:20
  106.6 2.8 %copy-start.1 = (bf16[2048,1536]{1,0:T(8,128)(2,1)S(1)}, bf16[2048,1536]{1,0:T(8,128)(2,1)}, u32[]{:S(2)}) copy-start(bf16[2048,1536]{1,0:T(8,128)(2,1)} %get-tuple-element.36.w_qkv) | copy-start | bytes 18874372
  109.4 2.2 copy-start.3
  111.6 3.3 %copy-start.9 = (bf16[128,1536]{1,0:T(8,128)(2,1)S(1)}, bf16[128,1536]{1,0:T(8,128)(2,1)}, u32[]{:S(2)}) copy-start(bf16[128,1536]{1,0:T(8,128)(2,1)} %copy-done.8) | copy-start | bytes 1179652
  111.6 3.4 %copy-start.5 = (bf16[4,512,128]{2,1,0:T(8,128)(2,1)S(1)}, bf16[4,512,128]{2,1,0:T(8,128)(2,1)}, u32[]{:S(2)}) copy-start(bf16[4,512,128]{2,1,0:T(8,128)(2,1)} %copy-done.4) | copy-start | bytes 1572868
  120.8 5.0 %copy-start.7 = (bf16[128,1536]{1,0:T(8,128)(2,1)S(1)}, bf16[128,1536]{1,0:T(8,128)(2,1)}, u32[]{:S(2)}) copy-start(bf16[128,1536]{1,0:T(8,128)(2,1)} %copy-done.6) | copy-start | bytes 1179652
  120.8 16.6 %collective-permute-start.2 = (bf16[128,2048]{1,0:T(8,128)(2,1)S(1)}, bf16[128,2048]{1,0:T(8,128)(2,1)S(1)}, u32[]{:S(2)}, u32[]{:S(2)}) collective-permute-start(bf16[128,2048]{1,0:T(8,128)(2,1)S(1)} %get-tuple-element.50), channel_id=1, source_target_pairs={{16,0},{17,1},{18,2},{19,3},{20,4},{21,5},{22,6},{23,7},{24,8},{25... | collective-permute-start | bytes 1572872 | tf_op jit(solution)/shard_map/ppermute | solution.py:20
  130.5 1.7 copy-start.11
  130.5 16.6 %collective-permute-start.3 = (bf16[128,2048]{1,0:T(8,128)(2,1)S(1)}, bf16[128,2048]{1,0:T(8,128)(2,1)S(1)}, u32[]{:S(2)}, u32[]{:S(2)}) collective-permute-start(bf16[128,2048]{1,0:T(8,128)(2,1)S(1)} %get-tuple-element.56), channel_id=1, source_target_pairs={{16,0},{17,1},{18,2},{19,3},{20,4},{21,5},{22,6},{23,7},{24,8},{25... | collective-permute-start | bytes 1572872 | tf_op jit(solution)/shard_map/ppermute | solution.py:20
  133.3 1.2 copy-start.12
  133.5 13.6 %copy-start.13 = (bf16[2,128,2048]{2,1,0:T(8,128)(2,1)S(1)}, bf16[2,128,2048]{2,1,0:T(8,128)(2,1)}, u32[]{:S(2)}) copy-start(bf16[2,128,2048]{2,1,0:T(8,128)(2,1)} %param.6) | copy-start | bytes 3145732
  158.2 74.2 %copy-start.14 = (bf16[1,128,1536]{2,1,0:T(8,128)(2,1)S(1)}, bf16[1,128,1536]{2,1,0:T(8,128)(2,1)}, u32[]{:S(2)}) copy-start(bf16[1,128,1536]{2,1,0:T(8,128)(2,1)} %param.8) | copy-start | bytes 1179652
